TPU v7x, 32 devices: a whole 2x2x4 slice. The times are simulated.
32 devices in a mesh: dp: 8 (over z, y), mp: 4 (over x, core).
Axes of the slice: x: 2, y: 2, z: 4, core: 2. Of those that a mesh axis runs over, the one named last changes fastest.
Arguments:
- tokens_in: bfloat16 [8192, 768], P(('dp', 'mp')), may hold values from -6 to 6
- segments: int32 [8, 1024], P('dp'), may hold values from 0 to 15, never falling along the last dimension, each value on 1 to 128 neighbouring positions
- pairing: int32 [128], P('dp'), may hold values from 0 to 127, as said below
- drop_masks: int32 [2, 2, 8192, 768], P(None, None, ('dp', 'mp')), may hold values 0 or 1
- w_qkv: bfloat16 [2, 3, 768, 768], P(None, None, 'dp', 'mp'), may hold values from -0.21875 to 0.21875
- w_out: bfloat16 [2, 768, 768], P(None, ('mp', 'dp')), may hold values from -1.75 to 1.75
- w_in: bfloat16 [2, 768, 3072], P(None, 'dp', 'mp'), may hold values from -0.21875 to 0.21875
- w_back: bfloat16 [2, 3072, 768], P(None, ('mp', 'dp')), may hold values from -0.109375 to 0.109375
- b_in: bfloat16 [2, 3072], P(None, ('mp', 'dp')), may hold values from -0.59765625 to 0.59765625
- biases: bfloat16 [2, 6, 768], P(None, None, 'dp'), may hold values from -0.59765625 to 0.59765625
- gains: bfloat16 [2, 2, 768], P(None, None, 'dp'), may hold values from 0.5 to 1.5
- pool_w: bfloat16 [768, 768], P('dp'), may hold values from -0.21875 to 0.21875
- pool_b: bfloat16 [768], P('dp'), may hold values from -0.59765625 to 0.59765625
Outputs:
- loss: float32 [128], P('dp')
- alignment: float32 [128], P('dp')
- uniformity: float32 [128], P('dp')
- grad_x: float32 [8192, 768], P(('dp', 'mp'))
- grad_w_qkv: float32 [2, 3, 768, 768], P(None, None, 'dp', 'mp')
- grad_w_out: float32 [2, 768, 768], P(None, ('mp', 'dp'))
- grad_w_in: float32 [2, 768, 3072], P(None, 'dp', 'mp')
- grad_w_back: float32 [2, 3072, 768], P(None, ('mp', 'dp'))
- grad_b_in: float32 [2, 3072], P(None, ('mp', 'dp'))
- grad_biases: float32 [2, 6, 768], P(None, None, ('dp', 'mp'))
- grad_gains: float32 [2, 2, 768], P(None, None, ('dp', 'mp'))
- grad_pool_w: float32 [768, 768], P('dp')
- grad_pool_b: float32 [768], P('dp')
Inputs may be any that keep to these rules, and one draw needn't show every extreme that they name: `segments`: along each row the segment numbers never fall, and each of the 16 numbers names a run of 1 to 128 positions. pairing[pairing[i]] = i and pairing[i] != i; pooled sentence i is sentence i % 16 of row i // 16.
All inputs are finite; a program needn't handle non-finite values. No bound on the sum of `drop_masks` on one device may be relied on, other than what follows from the above.
Results may differ from a plain program's by a relative error of at most 0.035.
Values may be sent and summed in bfloat16 or wider, within the bound.
A program may use at most 256 MiB of HBM per device.

v0:
```python
import jax
import jax.numpy as jnp
from jax import lax
from jax.sharding import PartitionSpec as P

HEAD_DIM = 64
SEGS = 16


TEMP = 0.05
EPS = 1e-06
KEEP = 0.9


def in_blocks(x, dim, count):
    dims = x.shape
    tiles = x.reshape(*dims[:dim], count, dims[dim] // count, *dims[dim + 1 :])
    return jnp.moveaxis(tiles, dim, 0)


def summed_on_arrival(x, axis, dim):
    count = lax.axis_size(axis)
    tiles = lax.all_to_all(in_blocks(x, dim, count), axis, 0, 0, tiled=True)
    return jnp.sum(tiles.astype(jnp.float32), axis=0)


def full_rows(shard_part):
    return lax.all_gather(shard_part, "mp", axis=0, tiled=True)


def branch_total(shard_part):
    return lax.psum_scatter(
        shard_part.astype(jnp.bfloat16), "mp", scatter_dimension=0, tiled=True
    ).astype(jnp.float32)


def input_total(shard_part):
    return lax.psum_scatter(
        shard_part.astype(jnp.bfloat16), "mp", scatter_dimension=0, tiled=True
    ).astype(jnp.float32)


def contract(left_side, right_side, left_dim, right_dim):
    return lax.dot_general(
        left_side,
        right_side,
        (((left_dim,), (right_dim,)), ((), ())),
        preferred_element_type=jnp.float32,
    )


def gelu_exact(values):
    return jax.nn.gelu(values, approximate=False)


def unit_rows(values):
    return values * lax.rsqrt(jnp.sum(values * values, 1, keepdims=True) + EPS)


def norm_forward(residual, gain_row, shift_row):
    center = jnp.mean(residual, 1)
    spread = lax.rsqrt(jnp.mean(residual * residual, 1) - center * center + EPS)
    normed = (residual - center[:, None]) * spread[:, None]
    return (normed * gain_row.astype(jnp.float32) + shift_row.astype(jnp.float32), normed, spread)


def norm_backward(grad_out, gain_row, normed, spread):
    scaled = grad_out * gain_row.astype(jnp.float32)
    first_mean = jnp.mean(scaled, 1)
    second_mean = jnp.mean(scaled * normed, 1)
    grad_in = spread[:, None] * (scaled - first_mean[:, None] - normed * second_mean[:, None])
    return (grad_in, jnp.sum(grad_out * normed, 0), jnp.sum(grad_out, 0))


def attend(proj_qkv, segments):
    rows_here, seq_len = segments.shape
    heads_here = proj_qkv.shape[2] // HEAD_DIM
    blocks = proj_qkv.reshape(3, rows_here, seq_len, heads_here, HEAD_DIM)
    block_rows = min(512, seq_len)
    score_scale = HEAD_DIM ** (-0.5)

    def one_row(row_items):
        queries, keys_row, values, labels = row_items
        out_blocks = []
        lse_blocks = []
        for offset in range(0, seq_len, block_rows):
            scores = (
                jnp.einsum(
                    "qhd,khd->hqk",
                    queries[offset : offset + block_rows],
                    keys_row,
                    preferred_element_type=jnp.float32,
                )
                * score_scale
            )
            same_doc = labels[offset : offset + block_rows, None] == labels[None, :]
            scores = jnp.where(same_doc[None], scores, -1000000000.0)
            row_peak = jnp.max(scores, -1, keepdims=True)
            exponent = jnp.exp(scores - row_peak)
            totals = jnp.sum(exponent, -1, keepdims=True)
            soft_probs = (exponent / totals).astype(jnp.bfloat16)
            out_blocks.append(
                jnp.einsum("hqk,khd->qhd", soft_probs, values, preferred_element_type=jnp.float32)
            )
            lse_blocks.append((row_peak + jnp.log(totals))[..., 0])
        return (jnp.concatenate(out_blocks, 0).astype(jnp.bfloat16), jnp.concatenate(lse_blocks, 1))

    attended, log_sums = lax.map(one_row, (blocks[0], blocks[1], blocks[2], segments))
    return (attended.reshape(rows_here * seq_len, heads_here * HEAD_DIM), log_sums)


def attend_back(proj_qkv, log_sums, grad_att, segments):
    rows_here, seq_len = segments.shape
    heads_here = proj_qkv.shape[2] // HEAD_DIM
    blocks = proj_qkv.reshape(3, rows_here, seq_len, heads_here, HEAD_DIM)
    grads_o = grad_att.reshape(rows_here, seq_len, heads_here, HEAD_DIM)
    block_rows = min(512, seq_len)
    score_scale = HEAD_DIM ** (-0.5)

    def one_row(row_items):
        queries, keys_row, values, labels, lse_row, grad_row = row_items
        grad_keys = jnp.zeros((seq_len, heads_here, HEAD_DIM), jnp.float32)
        grad_values = jnp.zeros((seq_len, heads_here, HEAD_DIM), jnp.float32)
        grad_queries = []
        for offset in range(0, seq_len, block_rows):
            q_block = queries[offset : offset + block_rows]
            scores = (
                jnp.einsum("qhd,khd->hqk", q_block, keys_row, preferred_element_type=jnp.float32)
                * score_scale
            )
            same_doc = labels[offset : offset + block_rows, None] == labels[None, :]
            scores = jnp.where(same_doc[None], scores, -1000000000.0)
            soft_probs = jnp.exp(scores - lse_row[:, offset : offset + block_rows, None])
            probs_low = soft_probs.astype(jnp.bfloat16)
            grad_block = grad_row[offset : offset + block_rows]
            grad_values = grad_values + jnp.einsum(
                "hqk,qhd->khd", probs_low, grad_block, preferred_element_type=jnp.float32
            )
            grad_probs = jnp.einsum(
                "qhd,khd->hqk", grad_block, values, preferred_element_type=jnp.float32
            )
            inner_sum = jnp.sum(soft_probs * grad_probs, -1, keepdims=True)
            grad_scores = (soft_probs * (grad_probs - inner_sum)).astype(jnp.bfloat16)
            grad_queries.append(
                jnp.einsum(
                    "hqk,khd->qhd", grad_scores, keys_row, preferred_element_type=jnp.float32
                )
                * score_scale
            )
            grad_keys = (
                grad_keys
                + jnp.einsum(
                    "hqk,qhd->khd", grad_scores, q_block, preferred_element_type=jnp.float32
                )
                * score_scale
            )
        return (jnp.concatenate(grad_queries, 0), grad_keys, grad_values)

    grad_parts = lax.map(one_row, (blocks[0], blocks[1], blocks[2], segments, log_sums, grads_o))
    width_here = heads_here * HEAD_DIM
    return (
        grad_parts[0].reshape(rows_here * seq_len, width_here),
        grad_parts[1].reshape(rows_here * seq_len, width_here),
        grad_parts[2].reshape(rows_here * seq_len, width_here),
    )


def head_slice(full_row, width_here):
    return lax.dynamic_slice_in_dim(full_row, lax.axis_index("mp") * width_here, width_here, 0)


def layer_forward(residual, weights, keep_masks, segments):
    w_three, w_proj, w_up, w_down, bias_up, shifts, scales = weights
    shifts32 = shifts.astype(jnp.float32)
    width_here = w_three.shape[2]
    rows_full = full_rows(residual.astype(jnp.bfloat16))
    proj_qkv = jnp.einsum("nd,kde->kne", rows_full, w_three, preferred_element_type=jnp.float32)
    query_bias = head_slice(shifts32[0], width_here)
    value_bias = head_slice(shifts32[1], width_here)
    added = jnp.stack([query_bias, jnp.zeros_like(query_bias), value_bias])
    proj_low = (proj_qkv + added[:, None, :]).astype(jnp.bfloat16)
    attended, log_sums = attend(proj_low, segments)
    mixed_out = (
        branch_total(jnp.dot(attended, w_proj, preferred_element_type=jnp.float32)) + shifts32[2]
    )
    summed = residual + keep_masks[0] * mixed_out / KEEP
    middle, normed_one, spread_one = norm_forward(summed, scales[0], shifts[3])
    middle_full = full_rows(middle.astype(jnp.bfloat16))
    hidden = jnp.dot(middle_full, w_up, preferred_element_type=jnp.float32) + bias_up.astype(
        jnp.float32
    )
    active = gelu_exact(hidden).astype(jnp.bfloat16)
    branch = branch_total(jnp.dot(active, w_down, preferred_element_type=jnp.float32)) + shifts32[4]
    summed_two = middle + keep_masks[1] * branch / KEEP
    output, normed_two, spread_two = norm_forward(summed_two, scales[1], shifts[5])
    saved_layer = (
        rows_full,
        proj_low,
        attended,
        log_sums,
        normed_one,
        spread_one,
        middle_full,
        hidden,
        active,
        normed_two,
        spread_two,
    )
    return (output, saved_layer)


def layer_backward(grad_out, weights, keep_masks, saved_layer, segments):
    w_three, w_proj, w_up, w_down, bias_up, shifts, scales = weights
    (
        rows_full,
        proj_low,
        attended,
        log_sums,
        normed_one,
        spread_one,
        middle_full,
        hidden,
        active,
        normed_two,
        spread_two,
    ) = saved_layer
    width_here = w_three.shape[2]
    grad_two, gain_two, shift_two = norm_backward(grad_out, scales[1], normed_two, spread_two)
    grad_branch = grad_two * keep_masks[1] / KEEP
    bias_down = jnp.sum(grad_branch, 0)
    branch_full = full_rows(grad_branch.astype(jnp.bfloat16))
    grad_active = contract(branch_full, w_down, 1, 1)
    grad_down = contract(active, branch_full, 0, 0)
    grad_hidden = jax.vjp(gelu_exact, hidden)[1](grad_active)[0].astype(jnp.bfloat16)
    grad_bias_up = jnp.sum(grad_hidden.astype(jnp.float32), 0)
    grad_up = contract(middle_full, grad_hidden, 0, 0)
    grad_middle = grad_two + input_total(contract(grad_hidden, w_up, 1, 1))
    grad_one, gain_one, shift_one = norm_backward(grad_middle, scales[0], normed_one, spread_one)
    grad_mixed = grad_one * keep_masks[0] / KEEP
    bias_proj = jnp.sum(grad_mixed, 0)
    mixed_full = full_rows(grad_mixed.astype(jnp.bfloat16))
    grad_proj = contract(attended, mixed_full, 0, 0)
    grad_attended = contract(mixed_full, w_proj, 1, 1).astype(jnp.bfloat16)
    grad_query, grad_key, grad_value = attend_back(proj_low, log_sums, grad_attended, segments)
    grad_qkv = jnp.stack([grad_query, grad_key, grad_value]).astype(jnp.bfloat16)
    grad_three = jnp.einsum("nd,kne->kde", rows_full, grad_qkv, preferred_element_type=jnp.float32)
    grad_rows = input_total(
        jnp.einsum("kne,kde->nd", grad_qkv, w_three, preferred_element_type=jnp.float32)
    )
    sums_qkv = jnp.sum(grad_qkv.astype(jnp.float32), 1)
    empty_row = jnp.zeros_like(bias_proj)
    start = lax.axis_index("mp") * width_here
    query_full = lax.dynamic_update_slice_in_dim(empty_row, sums_qkv[0], start, 0)
    value_full = lax.dynamic_update_slice_in_dim(empty_row, sums_qkv[2], start, 0)
    grad_shifts = jnp.stack([query_full, value_full, bias_proj, shift_one, bias_down, shift_two])
    grad_scales = jnp.stack([gain_one, gain_two])
    return (
        grad_one + grad_rows,
        (grad_three, grad_proj, grad_up, grad_down, grad_bias_up, grad_shifts, grad_scales),
    )


def fetch_layer(w_qkv, w_out, w_in, w_back, b_in, biases, gains, layer_index):
    return (
        lax.all_gather(w_qkv[layer_index], "dp", axis=1, tiled=True),
        lax.all_gather(w_out[layer_index], "dp", axis=0, tiled=True),
        lax.all_gather(w_in[layer_index], "dp", axis=0, tiled=True),
        lax.all_gather(w_back[layer_index], "dp", axis=0, tiled=True),
        lax.all_gather(b_in[layer_index], "dp", axis=0, tiled=True),
        lax.all_gather(biases[layer_index], "dp", axis=1, tiled=True),
        lax.all_gather(gains[layer_index], "dp", axis=1, tiled=True),
    )


def per_device(
    tokens_in,
    segments,
    pairing,
    drop_masks,
    w_qkv,
    w_out,
    w_in,
    w_back,
    b_in,
    biases,
    gains,
    pool_w,
    pool_b,
):
    layers = w_qkv.shape[0]
    local_rows = tokens_in.shape[0]
    rows_here, seq_len = segments.shape
    pooler = (
        lax.all_gather(pool_w, "dp", axis=0, tiled=True),
        lax.all_gather(pool_b, "dp", axis=0, tiled=True),
    )
    fetched = []
    saved_all = []
    residual = tokens_in.astype(jnp.float32)
    for layer_index in range(layers):
        weights = fetch_layer(w_qkv, w_out, w_in, w_back, b_in, biases, gains, layer_index)
        fetched.append(weights)
        residual, saved_layer = layer_forward(
            residual, weights, drop_masks[layer_index].astype(jnp.float32), segments
        )
        saved_all.append(saved_layer)
    numbers = jnp.arange(SEGS, dtype=jnp.int32)
    starts = jnp.sum((segments[:, None, :] < numbers[None, :, None]).astype(jnp.int32), 2)
    places = (starts + jnp.arange(rows_here, dtype=jnp.int32)[:, None] * seq_len).reshape(-1)
    local_places = places - lax.axis_index("mp") * local_rows
    inside = (local_places >= 0) & (local_places < local_rows)
    safe_places = jnp.clip(local_places, 0, local_rows - 1)
    cls_term = jnp.where(
        inside[:, None], residual[safe_places].astype(jnp.bfloat16).astype(jnp.float32), 0.0
    )
    cls_full = lax.psum(cls_term.astype(jnp.bfloat16), "mp")
    pool_full, pool_shift = pooler
    before = jnp.dot(cls_full, pool_full, preferred_element_type=jnp.float32) + pool_shift.astype(
        jnp.float32
    )
    pooled = jnp.tanh(before)
    normed_pool, unit_back = jax.vjp(unit_rows, pooled)
    unit_low = normed_pool.astype(jnp.bfloat16)
    everyone = lax.all_gather(unit_low, "dp", axis=0, tiled=True)
    pool_count = everyone.shape[0]
    pool_here = unit_low.shape[0]
    gram_raw = contract(unit_low, everyone, 1, 1)
    logits = gram_raw / TEMP
    own_ids = lax.axis_index("dp") * pool_here + jnp.arange(pool_here, dtype=jnp.int32)
    columns = jnp.arange(pool_count, dtype=jnp.int32)
    self_mask = columns[None, :] == own_ids[:, None]
    pair_mask = columns[None, :] == pairing[:, None]
    masked = jnp.where(self_mask, -1000000000.0, logits)
    row_peak = jnp.max(masked, 1, keepdims=True)
    exponent = jnp.exp(masked - row_peak)
    totals = jnp.sum(exponent, 1, keepdims=True)
    loss_rows = (
        row_peak[:, 0] + jnp.log(totals[:, 0]) - jnp.sum(jnp.where(pair_mask, logits, 0.0), 1)
    )
    squares_all = jnp.sum(jnp.square(everyone.astype(jnp.float32)), 1)
    squares_own = jnp.sum(jnp.square(unit_low.astype(jnp.float32)), 1)
    distance = squares_own[:, None] + squares_all[None, :] - 2.0 * gram_raw
    align_rows = jnp.sum(jnp.where(pair_mask, distance, 0.0), 1)
    unif_rows = jnp.log(
        jnp.sum(jnp.where(self_mask, 0.0, jnp.exp(-2.0 * distance)), 1) / (pool_count - 1)
    )
    grad_logits = exponent / totals - pair_mask.astype(jnp.float32)
    grad_raw = (grad_logits / TEMP).astype(jnp.bfloat16)
    grad_cols = summed_on_arrival(contract(grad_raw, unit_low, 0, 0).astype(jnp.bfloat16), "dp", 0)
    grad_unit = contract(grad_raw, everyone, 1, 0) + grad_cols
    grad_pooled = unit_back(grad_unit)[0]
    grad_before = (grad_pooled * (1.0 - pooled * pooled)).astype(jnp.bfloat16)
    grad_pool_w = contract(cls_full, grad_before, 0, 0)
    grad_pool_b = jnp.sum(grad_before.astype(jnp.float32), 0)
    grad_cls = contract(grad_before, pool_full, 1, 1)
    grad_resid = (
        jnp.zeros_like(residual).at[safe_places].add(jnp.where(inside[:, None], grad_cls, 0.0))
    )
    pool_grads = (
        lax.psum_scatter(grad_pool_w, "dp", scatter_dimension=0, tiled=True),
        lax.psum_scatter(grad_pool_b, "dp", scatter_dimension=0, tiled=True),
    )
    collected = [None] * layers
    small_parts = [None] * layers
    for layer_index in reversed(range(layers)):
        weights = (
            lax.all_gather(w_qkv[layer_index], "dp", axis=1, tiled=True),
            lax.all_gather(w_out[layer_index], "dp", axis=0, tiled=True),
            lax.all_gather(w_in[layer_index], "dp", axis=0, tiled=True),
            lax.all_gather(w_back[layer_index], "dp", axis=0, tiled=True),
            lax.all_gather(b_in[layer_index], "dp", axis=0, tiled=True),
            lax.all_gather(biases[layer_index], "dp", axis=1, tiled=True),
            lax.all_gather(gains[layer_index], "dp", axis=1, tiled=True),
        )
        grad_resid, layer_grads = layer_backward(
            grad_resid,
            weights,
            drop_masks[layer_index].astype(jnp.float32),
            saved_all[layer_index],
            segments,
        )
        collected[layer_index] = (
            lax.psum_scatter(layer_grads[0], "dp", scatter_dimension=1, tiled=True),
            lax.psum_scatter(layer_grads[1], "dp", scatter_dimension=0, tiled=True),
            lax.psum_scatter(layer_grads[2], "dp", scatter_dimension=0, tiled=True),
            lax.psum_scatter(layer_grads[3], "dp", scatter_dimension=0, tiled=True),
            lax.psum_scatter(layer_grads[4], "dp", scatter_dimension=0, tiled=True),
        )
        small_parts[layer_index] = (
            lax.psum_scatter(layer_grads[5], ("dp", "mp"), scatter_dimension=1, tiled=True),
            lax.psum_scatter(layer_grads[6], ("dp", "mp"), scatter_dimension=1, tiled=True),
        )
    return (
        loss_rows,
        align_rows,
        unif_rows,
        grad_resid,
        jnp.stack([shards[0] for shards in collected]),
        jnp.stack([shards[1] for shards in collected]),
        jnp.stack([shards[2] for shards in collected]),
        jnp.stack([shards[3] for shards in collected]),
        jnp.stack([shards[4] for shards in collected]),
        jnp.stack([shards[0] for shards in small_parts]),
        jnp.stack([shards[1] for shards in small_parts]),
        pool_grads[0],
        pool_grads[1],
    )


def solution(mesh):
    in_specs = (
        P(("dp", "mp"), None),
        P("dp", None),
        P("dp"),
        P(None, None, ("dp", "mp"), None),
        P(None, None, "dp", "mp"),
        P(None, ("mp", "dp"), None),
        P(None, "dp", "mp"),
        P(None, ("mp", "dp"), None),
        P(None, ("mp", "dp")),
        P(None, None, "dp"),
        P(None, None, "dp"),
        P("dp", None),
        P("dp"),
    )
    out_specs = (
        P("dp"),
        P("dp"),
        P("dp"),
        P(("dp", "mp"), None),
        P(None, None, "dp", "mp"),
        P(None, ("mp", "dp"), None),
        P(None, "dp", "mp"),
        P(None, ("mp", "dp"), None),
        P(None, ("mp", "dp")),
        P(None, None, ("dp", "mp")),
        P(None, None, ("dp", "mp")),
        P("dp", None),
        P("dp"),
    )
    return jax.shard_map(
        per_device, mesh=mesh, in_specs=in_specs, out_specs=out_specs, check_vma=False
    )
```

profile of v0, /device:TPU:0, one launch (start us, length us, event | category | flops | bytes accessed | tf_op | source)
XLA Modules:
  0.0 1524.5 jit_solution(8137650180169618806)
XLA Ops:
  11.6 38.6 %all-gather = bf16[1,3,768,192]{3,1,0,2:T(4,128)(2,1)S(1)} all-gather(bf16[1,3,96,192]{3,1,0,2:T(4,128)(2,1)S(1)} %copy.76), channel_id=2, replica_groups=mesh['dp'=8,'mp'=4] {'dp'}, dimensions={2}, use_global_device_ids=true | all-gather | bytes 995328 | tf_op jit(solution)/shard_map/all_gather | solution.py:265
  52.4 31.1 %all-gather.8 = bf16[1,6,768]{1,0,2:T(2,128)(2,1)S(1)} all-gather(bf16[1,6,96]{1,0,2:T(2,128)(2,1)S(1)} %copy.80), channel_id=10, replica_groups=mesh['dp'=8,'mp'=4] {'dp'}, dimensions={2}, use_global_device_ids=true | all-gather | bytes 10368 | tf_op jit(solution)/shard_map/all_gather | solution.py:270
  83.5 30.9 %all-gather.1 = bf16[1,6,768]{1,0,2:T(2,128)(2,1)S(1)} all-gather(bf16[1,6,96]{1,0,2:T(2,128)(2,1)S(1)} %copy.77), channel_id=3, replica_groups=mesh['dp'=8,'mp'=4] {'dp'}, dimensions={2}, use_global_device_ids=true | all-gather | bytes 10368 | tf_op jit(solution)/shard_map/all_gather | solution.py:270
  129.2 31.0 %all-gather.2 = bf16[1,192,768]{2,1,0:T(8,128)(2,1)S(1)} all-gather(bf16[1,24,768]{2,1,0:T(8,128)(2,1)S(1)} %get-tuple-element.281), channel_id=4, replica_groups=mesh['dp'=8,'mp'=4] {'dp'}, dimensions={1}, use_global_device_ids=true | all-gather | bytes 331776 | tf_op jit(solution)/shard_map/all_gather | solution.py:266
  180.3 31.5 %all-gather.3 = bf16[1,2,768]{1,0,2:T(2,128)(2,1)S(1)} all-gather(bf16[1,2,96]{1,0,2:T(2,128)(2,1)S(1)} %copy.78), channel_id=5, replica_groups=mesh['dp'=8,'mp'=4] {'dp'}, dimensions={2}, use_global_device_ids=true | all-gather | bytes 3456 | tf_op jit(solution)/shard_map/all_gather | solution.py:271
  240.1 21.0 %all-reduce.12 = (bf16[768]{0:T(1024)(128)(2,1)}, bf16[768]{0:T(1024)(128)(2,1)}, bf16[768]{0:T(1024)(128)(2,1)}) all-reduce(bf16[768]{0:T(1024)(128)(2,1)} %dynamic-update-slice, bf16[768]{0:T(1024)(128)(2,1)} %dynamic-update-slice.1, bf16[768]{0:T(1024)(128)(2,1)} %dynamic-update-slice.2), channel_id=7, replica_groups=mesh['dp'=8,'mp'=4] {'dp'}, use_global_device_ids=true, to_apply=%add | all-reduce | flops 2304 | bytes 9216
  273.6 18.9 %all-gather.48.cloned.1.call-done = bf16[1,768,768]{2,1,0:T(8,128)(2,1)} async-done(((bf16[1,96,768]{2,1,0:T(8,128)(2,1)}), bf16[1,768,768]{2,1,0:T(8,128)(2,1)}) %all-gather.48.cloned.1.call-update) | async-done | bytes 1179664 | tf_op jit(solution)/shard_map/all_gather | solution.py:268
  296.8 26.8 %reduce-scatter.28.cloned.1.call-done = bf16[256,768]{1,0:T(8,128)(2,1)} async-done(((bf16[1024,768]{1,0:T(8,128)(2,1)}), bf16[256,768]{1,0:T(8,128)(2,1)}) %reduce-scatter.28.cloned.1.call-update) | async-done | bytes 393232 | tf_op jit(solution)/shard_map/reduce_scatter | solution.py:32
  328.3 38.8 %all-gather.7 = bf16[1,3,768,192]{3,1,0,2:T(4,128)(2,1)} all-gather(bf16[1,3,96,192]{3,1,0,2:T(4,128)(2,1)S(1)} %copy.79), channel_id=9, replica_groups=mesh['dp'=8,'mp'=4] {'dp'}, dimensions={2}, use_global_device_ids=true | all-gather | bytes 995328 | tf_op jit(solution)/shard_map/all_gather | solution.py:265
  370.6 33.3 %all-gather.9 = bf16[1,192,768]{2,1,0:T(8,128)(2,1)} all-gather(bf16[1,24,768]{2,1,0:T(8,128)(2,1)} %get-tuple-element.282), channel_id=11, replica_groups=mesh['dp'=8,'mp'=4] {'dp'}, dimensions={1}, use_global_device_ids=true | all-gather | bytes 331776 | tf_op jit(solution)/shard_map/all_gather | solution.py:266
  421.7 31.6 %all-gather.10 = bf16[1,2,768]{1,0,2:T(2,128)(2,1)S(1)} all-gather(bf16[1,2,96]{1,0,2:T(2,128)(2,1)S(1)} %copy.81), channel_id=12, replica_groups=mesh['dp'=8,'mp'=4] {'dp'}, dimensions={2}, use_global_device_ids=true | all-gather | bytes 3456 | tf_op jit(solution)/shard_map/all_gather | solution.py:271
  469.6 17.9 %all-gather.34.cloned.1.call-done = bf16[1024,768]{1,0:T(8,128)(2,1)} async-done(((bf16[256,768]{1,0:T(8,128)(2,1)}), bf16[1024,768]{1,0:T(8,128)(2,1)}) %all-gather.34.cloned.1.call-update) | async-done | bytes 1572880 | tf_op jit(solution)/shard_map/all_gather | solution.py:28
  498.7 32.6 %all-gather.52.cloned.1.call-done = bf16[1,768,768]{2,1,0:T(8,128)(2,1)} async-done(((bf16[1,96,768]{2,1,0:T(8,128)(2,1)}), bf16[1,768,768]{2,1,0:T(8,128)(2,1)}) %all-gather.52.cloned.1.call-update) | async-done | bytes 1179664 | tf_op jit(solution)/shard_map/all_gather | solution.py:268
  538.6 23.8 %reduce-scatter.32.cloned.1.call-done = bf16[256,768]{1,0:T(8,128)(2,1)} async-done(((bf16[1024,768]{1,0:T(8,128)(2,1)}), bf16[256,768]{1,0:T(8,128)(2,1)}) %reduce-scatter.32.cloned.1.call-update) | async-done | bytes 393232 | tf_op jit(solution)/shard_map/reduce_scatter | solution.py:32
  581.0 30.8 %all_gather.105 = bf16[128,768]{1,0:T(8,128)(2,1)S(1)} all-gather(bf16[16,768]{1,0:T(8,128)(2,1)S(1)} %get-tuple-element.248), channel_id=1, replica_groups=mesh['dp'=8,'mp'=4] {'dp'}, dimensions={0}, use_global_device_ids=true | all-gather | bytes 221184 | tf_op jit(solution)/shard_map/all_gather | solution.py:324
  638.4 17.7 %all-gather.38.cloned.1.call-done = bf16[1024,768]{1,0:T(8,128)(2,1)} async-done(((bf16[256,768]{1,0:T(8,128)(2,1)}), bf16[1024,768]{1,0:T(8,128)(2,1)}) %all-gather.38.cloned.1.call-update) | async-done | bytes 1572880 | tf_op jit(solution)/shard_map/all_gather | solution.py:28
  666.6 28.0 %reduce-scatter.34.cloned.1.call-done = bf16[256,768]{1,0:T(8,128)(2,1)} async-done(((bf16[1024,768]{1,0:T(8,128)(2,1)}), bf16[256,768]{1,0:T(8,128)(2,1)}) %reduce-scatter.34.cloned.1.call-update) | async-done | bytes 393232 | tf_op jit(solution)/shard_map/reduce_scatter | solution.py:38
  701.6 18.1 %all-gather.40.cloned.1.call-done = bf16[1024,768]{1,0:T(8,128)(2,1)} async-done(((bf16[256,768]{1,0:T(8,128)(2,1)}), bf16[1024,768]{1,0:T(8,128)(2,1)}) %all-gather.40.cloned.1.call-update) | async-done | bytes 1572880 | tf_op jit(solution)/shard_map/all_gather | solution.py:28
  740.7 28.2 %reduce-scatter.36.cloned.1.call-done = bf16[256,768]{1,0:T(8,128)(2,1)} async-done(((bf16[1024,768]{1,0:T(8,128)(2,1)}), bf16[256,768]{1,0:T(8,128)(2,1)}) %reduce-scatter.36.cloned.1.call-update) | async-done | bytes 393232 | tf_op jit(solution)/shard_map/reduce_scatter | solution.py:38
  773.6 19.4 %all-gather.42.cloned.1.call-done = bf16[1024,768]{1,0:T(8,128)(2,1)} async-done(((bf16[256,768]{1,0:T(8,128)(2,1)}), bf16[1024,768]{1,0:T(8,128)(2,1)}) %all-gather.42.cloned.1.call-update) | async-done | bytes 1572880 | tf_op jit(solution)/shard_map/all_gather | solution.py:28
  803.3 28.3 %reduce-scatter.38.cloned.1.call-done = bf16[256,768]{1,0:T(8,128)(2,1)} async-done(((bf16[1024,768]{1,0:T(8,128)(2,1)}), bf16[256,768]{1,0:T(8,128)(2,1)}) %reduce-scatter.38.cloned.1.call-update) | async-done | bytes 393232 | tf_op jit(solution)/shard_map/reduce_scatter | solution.py:38
  929.8 35.5 %all-reduce.11 = (f32[768]{0:T(1024)S(1)}, f32[768]{0:T(1024)S(1)}, f32[768]{0:T(1024)S(1)}) all-reduce(f32[768]{0:T(1024)S(1)} %copy-done.114, f32[768]{0:T(1024)S(1)} %copy-done.115, f32[768]{0:T(1024)S(1)} %copy-done.106), channel_id=33, replica_groups=mesh['dp'=8,'mp'=4] {'dp'}, use_global_device_ids=true, to_apply=%region_60.61.clone | all-reduce | flops 2304 | bytes 18432
  966.7 33.5 %reduce-scatter.52.cloned.1.call-done = f32[96,768]{1,0:T(8,128)} async-done(((f32[768,768]{1,0:T(8,128)}), f32[96,768]{1,0:T(8,128)}) %reduce-scatter.52.cloned.1.call-update) | async-done | bytes 294928 | tf_op jit(solution)/shard_map/reduce_scatter | solution.py:386
  1000.2 71.5 %reduce-scatter.50.cloned.1.call-done = f32[96,768]{1,0:T(8,128)} async-done(((f32[768,768]{1,0:T(8,128)}), f32[96,768]{1,0:T(8,128)}) %reduce-scatter.50.cloned.1.call-update) | async-done | bytes 294928 | tf_op jit(solution)/shard_map/reduce_scatter | solution.py:386
  1073.6 69.6 %reduce-scatter.48.cloned.1.call-done = f32[96,768]{1,0:T(8,128)} async-done(((f32[768,768]{1,0:T(8,128)}), f32[96,768]{1,0:T(8,128)}) %reduce-scatter.48.cloned.1.call-update) | async-done | bytes 294928 | tf_op jit(solution)/shard_map/reduce_scatter | solution.py:385
  1143.2 71.4 %reduce-scatter.46.cloned.1.call-done = f32[96,768]{1,0:T(8,128)} async-done(((f32[768,768]{1,0:T(8,128)}), f32[96,768]{1,0:T(8,128)}) %reduce-scatter.46.cloned.1.call-update) | async-done | bytes 294928 | tf_op jit(solution)/shard_map/reduce_scatter | solution.py:385
  1217.2 40.5 %all-reduce.10 = (f32[6,768]{1,0:T(8,128)S(1)}, f32[6,768]{1,0:T(8,128)S(1)}, f32[2,768]{1,0:T(2,128)S(1)}, f32[2,768]{1,0:T(2,128)S(1)}) all-reduce(f32[6,768]{1,0:T(8,128)S(1)} %stack.165, f32[6,768]{1,0:T(8,128)S(1)} %stack.159, f32[2,768]{1,0:T(2,128)S(1)} %pad_maximum_fusion.16, ...), channel_id=35, replica_groups=mesh['dp'=8,'mp'=4] {'dp','mp'}, use_global_device_ids=true, to_apply=%region_72.73.clone | all-reduce | flops 12288 | bytes 98304
  1259.2 20.6 %reduce-scatter.44.cloned.1.call-done = f32[24,768]{1,0:T(8,128)} async-done(((f32[192,768]{1,0:T(8,128)}), f32[24,768]{1,0:T(8,128)}) %reduce-scatter.44.cloned.1.call-update) | async-done | bytes 73744 | tf_op jit(solution)/shard_map/reduce_scatter | solution.py:384
  1279.8 64.9 %reduce-scatter.42.cloned.1.call-done = f32[24,768]{1,0:T(8,128)} async-done(((f32[192,768]{1,0:T(8,128)}), f32[24,768]{1,0:T(8,128)}) %reduce-scatter.42.cloned.1.call-update) | async-done | bytes 73744 | tf_op jit(solution)/shard_map/reduce_scatter | solution.py:384
  1346.3 28.0 %reduce-scatter.40.cloned.1.call-done = bf16[256,768]{1,0:T(8,128)(2,1)} async-done(((bf16[1024,768]{1,0:T(8,128)(2,1)}), bf16[256,768]{1,0:T(8,128)(2,1)}) %reduce-scatter.40.cloned.1.call-update) | async-done | bytes 393232 | tf_op jit(solution)/shard_map/reduce_scatter | solution.py:38
  1376.2 69.0 %reduce-scatter.56.cloned.1.call-done = f32[96,576]{1,0:T(8,128)} async-done(((f32[768,576]{1,0:T(8,128)}), f32[96,576]{1,0:T(8,128)}) %reduce-scatter.56.cloned.1.call-update) | async-done | bytes 221200
  1447.7 69.5 %reduce-scatter.54.cloned.1.call-done = f32[96,768]{1,0:T(8,128)} async-done(((f32[768,768]{1,0:T(8,128)}), f32[96,768]{1,0:T(8,128)}) %reduce-scatter.54.cloned.1.call-update) | async-done | bytes 294928 | tf_op jit(solution)/shard_map/reduce_scatter | solution.py:360
  (578 shorter events, 352.7 us)
Async XLA Ops:
  8.0 153.6 %all-gather.28.cloned.1.call-start = ((), (), s32[]{:S(2)}) async-start(), calls=%async_computation.18 | async-start | bytes 1966080 | tf_op jit(solution)/shard_map/all_gather | solution.py:28
  8.7 215.7 %reduce-scatter.26.cloned.1.call-start = ((), (), s32[]{:S(2)}) async-start(), calls=%async_computation.19 | async-start | bytes 1966080 | tf_op jit(solution)/shard_map/reduce_scatter | solution.py:32
  178.4 84.1 %all-gather.46.cloned.1.call-start = ((), (), s32[]{:S(2)}) async-start(), calls=%async_computation.42 | async-start | bytes 1327104 | tf_op jit(solution)/shard_map/all_gather | solution.py:267
  179.2 83.3 %all-gather.30.cloned.1.call-start = ((), (), s32[]{:S(2)}) async-start(), calls=%async_computation.20 | async-start | bytes 1966080 | tf_op jit(solution)/shard_map/all_gather | solution.py:28
  229.4 63.1 %all-gather.48.cloned.1.call-start = ((), (), s32[]{:S(2)}) async-start(), calls=%async_computation.43 | async-start | bytes 1327104 | tf_op jit(solution)/shard_map/all_gather | solution.py:268
  231.2 92.4 %reduce-scatter.28.cloned.1.call-start = ((), (), s32[]{:S(2)}) async-start(), calls=%async_computation.21 | async-start | bytes 1966080 | tf_op jit(solution)/shard_map/reduce_scatter | solution.py:32
  296.8 107.1 %all-gather.32.cloned.1.call-start = ((), (), s32[]{:S(2)}) async-start(), calls=%async_computation.22 | async-start | bytes 1966080 | tf_op jit(solution)/shard_map/all_gather | solution.py:28
  327.2 137.9 %reduce-scatter.30.cloned.1.call-start = ((), (), s32[]{:S(2)}) async-start(), calls=%async_computation.23 | async-start | bytes 1966080 | tf_op jit(solution)/shard_map/reduce_scatter | solution.py:32
  419.6 50.0 %all-gather.50.cloned.1.call-start = ((), (), s32[]{:S(2)}) async-start(), calls=%async_computation.44 | async-start | bytes 1327104 | tf_op jit(solution)/shard_map/all_gather | solution.py:267
  420.3 67.1 %all-gather.34.cloned.1.call-start = ((), (), s32[]{:S(2)}) async-start(), calls=%async_computation.24 | async-start | bytes 1966080 | tf_op jit(solution)/shard_map/all_gather | solution.py:28
  468.7 62.6 %all-gather.52.cloned.1.call-start = ((), (), s32[]{:S(2)}) async-start(), calls=%async_computation.45 | async-start | bytes 1327104 | tf_op jit(solution)/shard_map/all_gather | solution.py:268
  469.3 93.2 %reduce-scatter.32.cloned.1.call-start = ((), (), s32[]{:S(2)}) async-start(), calls=%async_computation.25 | async-start | bytes 1966080 | tf_op jit(solution)/shard_map/reduce_scatter | solution.py:32
  535.6 43.4 %all-gather.36.cloned.1.call-start = ((), (), s32[]{:S(2)}) async-start(), calls=%async_computation.26 | async-start | bytes 1327104 | tf_op jit(solution)/shard_map/all_gather | solution.py:294
  536.2 119.9 %all-gather.38.cloned.1.call-start = ((), (), s32[]{:S(2)}) async-start(), calls=%async_computation.27 | async-start | bytes 1966080 | tf_op jit(solution)/shard_map/all_gather | solution.py:28
  638.4 56.3 %reduce-scatter.34.cloned.1.call-start = ((), (), s32[]{:S(2)}) async-start(), calls=%async_computation.28 | async-start | bytes 1966080 | tf_op jit(solution)/shard_map/reduce_scatter | solution.py:38
  666.4 53.3 %all-gather.40.cloned.1.call-start = ((), (), s32[]{:S(2)}) async-start(), calls=%async_computation.29 | async-start | bytes 1966080 | tf_op jit(solution)/shard_map/all_gather | solution.py:28
  700.1 68.8 %reduce-scatter.36.cloned.1.call-start = ((), (), s32[]{:S(2)}) async-start(), calls=%async_computation.30 | async-start | bytes 1966080 | tf_op jit(solution)/shard_map/reduce_scatter | solution.py:38
  740.7 52.3 %all-gather.42.cloned.1.call-start = ((), (), s32[]{:S(2)}) async-start(), calls=%async_computation.31 | async-start | bytes 1966080 | tf_op jit(solution)/shard_map/all_gather | solution.py:28
  773.1 58.5 %reduce-scatter.38.cloned.1.call-start = ((), (), s32[]{:S(2)}) async-start(), calls=%async_computation.32 | async-start | bytes 1966080 | tf_op jit(solution)/shard_map/reduce_scatter | solution.py:38
  803.2 64.9 %all-gather.44.cloned.1.call-start = ((), (), s32[]{:S(2)}) async-start(), calls=%async_computation.33 | async-start | bytes 1966080 | tf_op jit(solution)/shard_map/all_gather | solution.py:28
  837.9 90.5 %reduce-scatter.58.cloned.1.call-start = ((), (), s32[]{:S(2)}) async-start(), calls=%async_computation.47 | async-start | bytes 2211840
  847.6 152.6 %reduce-scatter.52.cloned.1.call-start = ((), (), s32[]{:S(2)}) async-start(), calls=%async_computation.40 | async-start | bytes 2654208 | tf_op jit(solution)/shard_map/reduce_scatter | solution.py:386
  852.5 219.1 %reduce-scatter.50.cloned.1.call-start = ((), (), s32[]{:S(2)}) async-start(), calls=%async_computation.39 | async-start | bytes 2654208 | tf_op jit(solution)/shard_map/reduce_scatter | solution.py:386
  857.0 286.2 %reduce-scatter.48.cloned.1.call-start = ((), (), s32[]{:S(2)}) async-start(), calls=%async_computation.38 | async-start | bytes 2654208 | tf_op jit(solution)/shard_map/reduce_scatter | solution.py:385
  861.4 353.2 %reduce-scatter.46.cloned.1.call-start = ((), (), s32[]{:S(2)}) async-start(), calls=%async_computation.37 | async-start | bytes 2654208 | tf_op jit(solution)/shard_map/reduce_scatter | solution.py:385
  866.6 413.2 %reduce-scatter.44.cloned.1.call-start = ((), (), s32[]{:S(2)}) async-start(), calls=%async_computation.36 | async-start | bytes 663552 | tf_op jit(solution)/shard_map/reduce_scatter | solution.py:384
  868.0 476.7 %reduce-scatter.42.cloned.1.call-start = ((), (), s32[]{:S(2)}) async-start(), calls=%async_computation.35 | async-start | bytes 663552 | tf_op jit(solution)/shard_map/reduce_scatter | solution.py:384
  886.4 487.9 %reduce-scatter.40.cloned.1.call-start = ((), (), s32[]{:S(2)}) async-start(), calls=%async_computation.34 | async-start | bytes 1966080 | tf_op jit(solution)/shard_map/reduce_scatter | solution.py:38
  898.6 546.7 %reduce-scatter.56.cloned.1.call-start = ((), (), s32[]{:S(2)}) async-start(), calls=%async_computation.46 | async-start | bytes 2211840
  908.6 608.6 %reduce-scatter.54.cloned.1.call-start = ((), (), s32[]{:S(2)}) async-start(), calls=%async_computation.41 | async-start | bytes 2654208 | tf_op jit(solution)/shard_map/reduce_scatter | solution.py:360
  911.4 305.1 %copy-start.43 = (bf16[3,64,1024]{2,1,0:T(8,128)(2,1)S(1)}, bf16[3,64,1024]{2,1,0:T(8,128)(2,1)}, u32[]{:S(2)}) copy-start(bf16[3,64,1024]{2,1,0:T(8,128)(2,1)} %copy-done.42) | copy-start | bytes 1179652
  913.3 460.9 %copy-start.15 = (f32[256,768]{1,0:T(8,128)S(1)}, f32[256,768]{1,0:T(8,128)}, u32[]{:S(2)}) copy-start(f32[256,768]{1,0:T(8,128)} %copy-done.14) | copy-start | bytes 2359300
  (142 other events, 2673.4 us)
Sparse Core Ops, SparseCore 0:
  10.4 22.3 all-gather.27
  178.5 27.4 reduce-scatter.25
  296.9 26.6 reduce-scatter.27
  419.7 27.1 reduce-scatter.29
  535.7 26.6 reduce-scatter.31
  638.5 17.5 all-gather.37
  666.5 28.1 reduce-scatter.33
  773.2 19.6 all-gather.41
  803.3 28.1 reduce-scatter.37
Sparse Core Ops, SparseCore 1:
  181.3 41.1 all-gather.45
  229.4 19.1 all-gather.29
  250.9 41.5 all-gather.47
  327.3 19.5 all-gather.31
  422.8 40.9 all-gather.49
  468.8 18.6 all-gather.33
  489.8 41.5 all-gather.51
  538.3 40.0 all-gather.35
  700.2 19.5 all-gather.39
  740.8 28.1 reduce-scatter.35
  838.0 19.5 all-gather.43
  861.4 67.0 reduce-scatter.57
  931.8 68.3 reduce-scatter.51
  1003.7 67.9 reduce-scatter.49
  1075.2 67.9 reduce-scatter.47
  1146.7 67.8 reduce-scatter.45
  1218.5 61.2 reduce-scatter.43
  1283.4 61.2 reduce-scatter.41
  1347.1 27.1 reduce-scatter.39
  1378.2 67.0 reduce-scatter.55
  1449.2 67.9 reduce-scatter.53
where the time goes:
time: 1540 us; the launch traced here: 1520 us
  waiting for transfers between devices  775 us (50%)
  blocking collectives  418 us (27%)
  matrix products  148 us (10%)
  other arithmetic  91.6 us (6%)
  local copies, waits for them, and re-layouts  69.7 us (5%)
  between operations  19.3 us (1%)
    reduce_scatter x2, waiting for transfers between devices, per_device(): lax.psum_scatter(layer_grads[2], 'dp', scatter_dimension=0, tiled=True)  141 us
    reduce_scatter x4, waiting for transfers between devices, input_total(): lax.psum_scatter(shard_part.astype(jnp.bfloat16), 'mp', scatter_dimension...  112 us
    reduce_scatter x2, waiting for transfers between devices, per_device(): lax.psum_scatter(layer_grads[3], 'dp', scatter_dimension=0, tiled=True)  105 us
    unnamed x3, blocking collectives  97 us
    unnamed x32, waiting for transfers between devices  86.3 us
    reduce_scatter x2, waiting for transfers between devices, per_device(): lax.psum_scatter(layer_grads[1], 'dp', scatter_dimension=0, tiled=True)  85.5 us
    all_gather x2, blocking collectives, fetch_layer(): lax.all_gather(w_qkv[layer_index], 'dp', axis=1, tiled=True)  77.5 us
    all_gather x8, waiting for transfers between devices, full_rows(): return lax.all_gather(shard_part, 'mp', axis=0, tiled=True)  73.1 us
  transfers between devices with their start and end apart: 30, of which 21 were waited for; matrix products, arithmetic and copies ran while one was open for 12% of the time, Pallas kernels for 0%

commit v1 on v0

v1 whole, which is shorter than its diff:
```python
import functools

import jax
import jax.numpy as jnp
from jax import lax
from jax.experimental import pallas as pl
from jax.experimental.pallas import tpu as pltpu
from jax.sharding import Mesh
from jax.sharding import PartitionSpec as P

HEAD_DIM = 64
SEGS = 16
TEMP = 0.05
EPS = 1e-06
KEEP = 0.9
HALO = 128
MESH = pl.DeviceIdType.MESH
ANY = pl.BlockSpec(memory_space=pl.ANY)
VMEM = pl.BlockSpec(memory_space=pltpu.VMEM)
BF = jnp.bfloat16
F32 = jnp.float32
NZ = 4
NY = 2


def contract(left_side, right_side, left_dim, right_dim):
    return lax.dot_general(
        left_side,
        right_side,
        (((left_dim,), (right_dim,)), ((), ())),
        preferred_element_type=F32,
    )


def mm(a, b):
    return jnp.dot(a, b, preferred_element_type=F32)


def position():
    return tuple(lax.axis_index(name) for name in ("z", "y", "x", "c"))


def neighbours():
    x, c = lax.axis_index("x"), lax.axis_index("c")
    m = 2 * x + c
    left = {"x": jnp.where(c == 1, x, x - 1), "c": 1 - c}
    right = {"x": jnp.where(c == 0, x, x + 1), "c": 1 - c}
    return m, left, right


def signal(sem, device):
    pl.semaphore_signal(sem, inc=1, device_id=device, device_id_type=MESH)


def gather_kernel(nblk, *refs):
    ins = refs[:nblk]
    tok = refs[nblk]
    outs = refs[nblk + 1 : 2 * nblk + 1]
    halo = refs[2 * nblk + 1]
    zsend, xsend, ysend, csend, recv, own_sem, hsend, hrecv = refs[2 * nblk + 2 :]
    z, y, x, c = position()
    m, left, right = neighbours()
    up, down = z < NZ - 1, z > 0
    xdev, ydev, cdev = {"x": 1 - x}, {"y": 1 - y}, {"c": 1 - c}
    diag_halo = (m == 1) | (m == 2)
    diag_dev = {"x": 1 - x, "c": 1 - c}

    bar = pltpu.get_barrier_semaphore()
    signal(bar, xdev)
    signal(bar, ydev)
    signal(bar, cdev)

    @pl.when(up)
    def _():
        signal(bar, {"z": z + 1})

    @pl.when(down)
    def _():
        signal(bar, {"z": z - 1})

    @pl.when(diag_halo)
    def _():
        signal(bar, diag_dev)

    pl.semaphore_wait(
        bar, 3 + up.astype(jnp.int32) + down.astype(jnp.int32) + diag_halo.astype(jnp.int32)
    )

    def copy(b, src, slot, device, sem):
        return pltpu.make_async_remote_copy(
            src_ref=src,
            dst_ref=outs[b].at[slot],
            send_sem=sem,
            recv_sem=recv.at[(b, *slot)],
            device_id=device,
            device_id_type=MESH,
        )

    def arrived(b, slot):
        ref = outs[b].at[slot]
        pltpu.make_async_copy(ref, ref, recv.at[(b, *slot)]).wait()

    def halo_copies():
        return (
            (m > 0, pltpu.make_async_remote_copy(
                src_ref=tok.at[0:HALO], dst_ref=halo.at[1], send_sem=hsend.at[0], recv_sem=hrecv.at[1],
                device_id=left, device_id_type=MESH)),
            (m < 3, pltpu.make_async_remote_copy(
                src_ref=tok.at[tok.shape[0] - HALO :], dst_ref=halo.at[0], send_sem=hsend.at[1],
                recv_sem=hrecv.at[0], device_id=right, device_id_type=MESH)),
        )

    def x_first(b):
        return b % 2 == 0

    def fan_out(b, src, slot, k):
        copy(b, src, slot, xdev, xsend.at[b, k]).start()
        copy(b, src, slot, ydev, ysend.at[b, k]).start()
        copy(b, src, slot, cdev, csend.at[b, 0, k]).start()

    def z_events(b):
        src = ins[b]
        mine = (x, c, z, y)

        @pl.when(up)
        def _():
            copy(b, src, mine, {"z": z + 1}, zsend.at[b, 0]).start()

        @pl.when(down)
        def _():
            copy(b, src, mine, {"z": z - 1}, zsend.at[b, 1]).start()

        fan_out(b, src, mine, 0)
        pltpu.make_async_copy(src, outs[b].at[mine], own_sem.at[b]).start()

    def z_relay(b, d):
        @pl.when(z >= d)
        def _():
            slot = (x, c, z - d, y)
            arrived(b, slot)

            @pl.when(up)
            def _():
                copy(b, outs[b].at[slot], slot, {"z": z + 1}, zsend.at[b, 2 * d]).start()

            fan_out(b, outs[b].at[slot], slot, NZ - d)

        @pl.when(z < NZ - d)
        def _():
            slot = (x, c, z + d, y)
            arrived(b, slot)

            @pl.when(down)
            def _():
                copy(b, outs[b].at[slot], slot, {"z": z - 1}, zsend.at[b, 2 * d + 1]).start()

            fan_out(b, outs[b].at[slot], slot, d)

    def xy_relay(b, k):
        zp = lax.rem(z + k, NZ)
        sx, sy = (1 - x, c, zp, y), (x, c, zp, 1 - y)
        arrived(b, sx)
        if x_first(b):
            copy(b, outs[b].at[sx], sx, ydev, ysend.at[b, NZ + k]).start()
        copy(b, outs[b].at[sx], sx, cdev, csend.at[b, 1, k]).start()
        arrived(b, sy)
        if not x_first(b):
            copy(b, outs[b].at[sy], sy, xdev, xsend.at[b, NZ + k]).start()
        copy(b, outs[b].at[sy], sy, cdev, csend.at[b, 2, k]).start()

    def corner(b, k):
        zp = lax.rem(z + k, NZ)
        sd = (1 - x, c, zp, 1 - y)
        arrived(b, sd)
        copy(b, outs[b].at[sd], sd, cdev, csend.at[b, 3, k]).start()

    for cond, cp in halo_copies():
        pl.when(cond)(cp.start)

    for t in range(nblk + 2):
        if t < nblk:
            z_events(t)
            for d in range(1, NZ):
                z_relay(t, d)
        if 0 <= t - 1 < nblk:
            for k in range(NZ):
                xy_relay(t - 1, k)
        if 0 <= t - 2 < nblk:
            for k in range(NZ):
                corner(t - 2, k)

    for b in range(nblk):
        src = ins[b]
        mine = (x, c, z, y)
        pltpu.make_async_copy(src, outs[b].at[mine], own_sem.at[b]).wait()
        for k in range(NZ):
            zp = lax.rem(z + k, NZ)
            for xp in (x, 1 - x):
                for yp in (y, 1 - y):
                    arrived(b, (xp, 1 - c, zp, yp))
            copy(b, src, mine, xdev, xsend.at[b, k]).wait_send()
            copy(b, src, mine, ydev, ysend.at[b, k]).wait_send()
            if x_first(b):
                copy(b, src, mine, ydev, ysend.at[b, NZ + k]).wait_send()
            else:
                copy(b, src, mine, xdev, xsend.at[b, NZ + k]).wait_send()
            for kind in range(4):
                copy(b, src, mine, cdev, csend.at[b, kind, k]).wait_send()
        for d in range(NZ):

            @pl.when(up & (z >= d))
            def _():
                copy(b, src, mine, {"z": z + 1}, zsend.at[b, 2 * d]).wait_send()

            @pl.when(down & (z < NZ - d))
            def _():
                copy(b, src, mine, {"z": z - 1}, zsend.at[b, 2 * d + 1]).wait_send()

    (has_left, to_left), (has_right, to_right) = halo_copies()
    pl.when(has_left)(to_left.wait_send)
    pl.when(has_right)(to_right.wait_send)
    pl.when(has_left)(to_right.wait_recv)
    pl.when(has_right)(to_left.wait_recv)


def gather_all(blocks, tokens):
    nblk = len(blocks)
    outs = [jax.ShapeDtypeStruct((2, 2, NZ, NY, *b.shape), b.dtype) for b in blocks]
    dma = pltpu.SemaphoreType.DMA
    res = pl.pallas_call(
        functools.partial(gather_kernel, nblk),
        out_shape=outs + [jax.ShapeDtypeStruct((2, HALO, tokens.shape[1]), tokens.dtype)],
        in_specs=[ANY] * (nblk + 1),
        out_specs=[ANY] * (nblk + 1),
        scratch_shapes=[
            dma((nblk, 2 * NZ)),
            dma((nblk, 2 * NZ)),
            dma((nblk, 2 * NZ)),
            dma((nblk, 4, NZ)),
            dma((nblk, 2, 2, NZ, NY)),
            dma((nblk,)),
            dma((2,)),
            dma((2,)),
        ],
        compiler_params=pltpu.CompilerParams(collective_id=1, has_side_effects=True),
        name="gather_params",
    )(*blocks, tokens)
    return res[:nblk], res[nblk]


def halo_kernel(a_ref, o_ref, ssem, rsem):
    m, left, right = neighbours()
    has_left, has_right = m > 0, m < 3
    bar = pltpu.get_barrier_semaphore()
    pl.when(has_left)(lambda: signal(bar, left))
    pl.when(has_right)(lambda: signal(bar, right))
    pl.semaphore_wait(bar, has_left.astype(jnp.int32) + has_right.astype(jnp.int32))
    to_left = pltpu.make_async_remote_copy(
        src_ref=a_ref.at[0], dst_ref=o_ref.at[1], send_sem=ssem.at[0], recv_sem=rsem.at[1],
        device_id=left, device_id_type=MESH)
    to_right = pltpu.make_async_remote_copy(
        src_ref=a_ref.at[1], dst_ref=o_ref.at[0], send_sem=ssem.at[1], recv_sem=rsem.at[0],
        device_id=right, device_id_type=MESH)
    pl.when(has_left)(to_left.start)
    pl.when(has_right)(to_right.start)

    @pl.when(~has_left)
    def _():
        o_ref[0] = jnp.zeros_like(o_ref[0])

    @pl.when(~has_right)
    def _():
        o_ref[1] = jnp.zeros_like(o_ref[1])

    pl.when(has_left)(to_left.wait_send)
    pl.when(has_right)(to_right.wait_send)
    pl.when(has_left)(to_right.wait_recv)
    pl.when(has_right)(to_left.wait_recv)


def swap_halos(to_left, to_right, cid):
    both = jnp.stack([to_left, to_right])
    dma = pltpu.SemaphoreType.DMA
    return pl.pallas_call(
        halo_kernel,
        out_shape=jax.ShapeDtypeStruct(both.shape, both.dtype),
        in_specs=[VMEM],
        out_specs=VMEM,
        scratch_shapes=[dma((2,)), dma((2,))],
        compiler_params=pltpu.CompilerParams(collective_id=cid, has_side_effects=True),
        name=f"halo_{cid}",
    )(both)


def pooled_kernel(a_ref, o_ref, part, s1, r1, s2, r2):
    z, y, x, c = position()
    mates = ({"x": 1 - x}, {"c": 1 - c}, {"x": 1 - x, "c": 1 - c})
    peers = []
    for k in range(NZ):
        for flip in range(NY):
            if k or flip:
                peers.append((k * NY + flip, k, flip))

    def peer(k, flip):
        return {"z": lax.rem(z + k, NZ), "y": y if flip == 0 else 1 - y}

    bar = pltpu.get_barrier_semaphore()
    for dev in mates:
        signal(bar, dev)
    for _, k, flip in peers:
        signal(bar, peer(k, flip))
    pl.semaphore_wait(bar, len(mates) + len(peers))
    first = [
        pltpu.make_async_remote_copy(
            src_ref=a_ref, dst_ref=part.at[i], send_sem=s1.at[i], recv_sem=r1.at[i],
            device_id=dev, device_id_type=MESH)
        for i, dev in enumerate(mates)
    ]
    for cp in first:
        cp.start()
    for cp in first:
        cp.wait()
    row = a_ref[...].astype(F32)
    for i in range(len(mates)):
        row = row + part[i].astype(F32)
    here = o_ref.at[z, y]
    here[...] = row.astype(BF)
    second = [
        pltpu.make_async_remote_copy(
            src_ref=here, dst_ref=here, send_sem=s2.at[i], recv_sem=r2.at[i],
            device_id=peer(k, flip), device_id_type=MESH)
        for i, k, flip in peers
    ]
    for cp in second:
        cp.start()
    for cp in second:
        cp.wait_send()
    for i, k, flip in peers:
        there = o_ref.at[lax.rem(z + NZ - k, NZ), y if flip == 0 else 1 - y]
        pltpu.make_async_copy(there, there, r2.at[i]).wait()


def share_pooled(rows):
    dma = pltpu.SemaphoreType.DMA
    return pl.pallas_call(
        pooled_kernel,
        out_shape=jax.ShapeDtypeStruct((NZ, NY, *rows.shape), rows.dtype),
        in_specs=[VMEM],
        out_specs=VMEM,
        scratch_shapes=[
            pltpu.VMEM((3, *rows.shape), rows.dtype),
            dma((3,)), dma((3,)), dma((NZ * NY,)), dma((NZ * NY,)),
        ],
        compiler_params=pltpu.CompilerParams(collective_id=9, has_side_effects=True),
        name="share_pooled",
    )(rows)


def reduce_kernel(nblk, *refs):
    ins = refs[:nblk]
    outs = refs[nblk : 2 * nblk]
    scr = refs[2 * nblk :]
    own, rc, p1x, p1y, p2x, p2y, q, zu, zd = (scr[i * nblk : (i + 1) * nblk] for i in range(9))
    csend, crecv, lsem, s1, r1, s2, r2, zs, zr = scr[9 * nblk :]
    z, y, x, c = position()
    up, down = z < NZ - 1, z > 0
    xdev, ydev, cdev = {"x": 1 - x}, {"y": 1 - y}, {"c": 1 - c}

    bar = pltpu.get_barrier_semaphore()
    signal(bar, xdev)
    signal(bar, ydev)
    signal(bar, cdev)
    pl.when(up)(lambda: signal(bar, {"z": z + 1}))
    pl.when(down)(lambda: signal(bar, {"z": z - 1}))
    pl.semaphore_wait(bar, 3 + up.astype(jnp.int32) + down.astype(jnp.int32))

    def remote(src, dst, ss, rs, dev):
        return pltpu.make_async_remote_copy(
            src_ref=src, dst_ref=dst, send_sem=ss, recv_sem=rs, device_id=dev, device_id_type=MESH)

    def add(a, b):
        return (a.astype(F32) + b.astype(F32)).astype(a.dtype)

    def core_copies(b):
        return [remote(ins[b].at[i, 1 - c], rc[b].at[i], csend.at[b, i], crecv.at[b, i], cdev) for i in range(2)]

    def local_copies(b):
        return [pltpu.make_async_copy(ins[b].at[i, c], own[b].at[i], lsem.at[b, i]) for i in range(2)]

    def half(b):
        return ins[b].shape[4] // 2

    def first_x(b):
        h = half(b)
        return remote(own[b].at[1 - x, :, :, 0:h], p1x[b], s1.at[b, 0], r1.at[b, 0], xdev)

    def first_y(b):
        h = half(b)
        return remote(own[b].at[:, :, 1 - y, h:], p1y[b], s1.at[b, 1], r1.at[b, 1], ydev)

    def second_y(b):
        h = half(b)
        return remote(own[b].at[x, :, 1 - y, 0:h], p2y[b], s2.at[b, 0], r2.at[b, 0], ydev)

    def second_x(b):
        h = half(b)
        return remote(own[b].at[1 - x, :, y, h:], p2x[b], s2.at[b, 1], r2.at[b, 1], xdev)

    def stage0(b):
        for cp in core_copies(b) + local_copies(b):
            cp.start()

    def stage1(b):
        for cp in core_copies(b):
            cp.wait_recv()
        for cp in local_copies(b):
            cp.wait()

        @pl.loop(0, NZ)
        def _(k):
            for i in range(2):
                own[b][i, k] = add(own[b][i, k], rc[b][i, k])

        first_x(b).start()
        first_y(b).start()

    def stage2(b):
        h = half(b)
        first_x(b).wait_recv()
        first_y(b).wait_recv()

        @pl.loop(0, NZ)
        def _(k):
            a = own[b].at[x, k, :, 0:h]
            a[...] = add(a[...], p1x[b][k])
            for i in range(2):
                a = own[b].at[i, k, y, h:]
                a[...] = add(a[...], p1y[b][i, k])

        second_y(b).start()
        second_x(b).start()

    def zcopy(b, j, upward):
        if upward:
            return remote(q[b].at[0, z + j], zu[b].at[z + j], zs.at[b, 0, j], zr.at[b, 0, j], {"z": z + 1})
        return remote(q[b].at[1, z - j], zd[b].at[z - j], zs.at[b, 1, j], zr.at[b, 1, j], {"z": z - 1})

    def zarrived(b, j, upward):
        if upward:
            ref = zu[b].at[z + j]
            pltpu.make_async_copy(ref, ref, zr.at[b, 0, j + 1]).wait()
        else:
            ref = zd[b].at[z - j]
            pltpu.make_async_copy(ref, ref, zr.at[b, 1, j + 1]).wait()

    def stage3(b):
        h = half(b)
        second_y(b).wait_recv()
        second_x(b).wait_recv()

        @pl.loop(0, NZ)
        def _(k):
            lo = add(own[b][x, k, y, 0:h], p2y[b][k])
            hi = add(own[b][x, k, y, h:], p2x[b][k])
            for d in range(2):
                q[b][d, k, 0:h] = lo
                q[b][d, k, h:] = hi

        for j in range(NZ - 1, 0, -1):

            @pl.when(z + j < NZ)
            def _():
                @pl.when(down)
                def _():
                    zarrived(b, j, True)
                    q[b][0, z + j] = add(q[b][0, z + j], zu[b][z + j])

                zcopy(b, j, True).start()

            @pl.when(z - j >= 0)
            def _():
                @pl.when(up)
                def _():
                    zarrived(b, j, False)
                    q[b][1, z - j] = add(q[b][1, z - j], zd[b][z - j])

                zcopy(b, j, False).start()

    def stage4(b):
        outs[b][...] = q[b][0, z].astype(F32)

        @pl.when(down)
        def _():
            zarrived(b, 0, True)
            outs[b][...] += zu[b][z].astype(F32)

        @pl.when(up)
        def _():
            zarrived(b, 0, False)
            outs[b][...] += zd[b][z].astype(F32)

    for t in range(nblk + 4):
        if t < nblk:
            stage0(t)
        if 0 <= t - 1 < nblk:
            stage1(t - 1)
        if 0 <= t - 2 < nblk:
            stage2(t - 2)
        if 0 <= t - 3 < nblk:
            stage3(t - 3)
        if 0 <= t - 4 < nblk:
            stage4(t - 4)

    for b in range(nblk):
        for cp in core_copies(b):
            cp.wait_send()
        for cp in (first_x(b), first_y(b), second_y(b), second_x(b)):
            cp.wait_send()
        for j in range(1, NZ):
            pl.when(z + j < NZ)(lambda: zcopy(b, j, True).wait_send())
            pl.when(z - j >= 0)(lambda: zcopy(b, j, False).wait_send())


def reduce_all(blocks):
    nblk = len(blocks)
    dma = pltpu.SemaphoreType.DMA

    def scratch(shape_of):
        return [pltpu.VMEM(shape_of(*b.shape[4:]), b.dtype) for b in blocks]

    return pl.pallas_call(
        functools.partial(reduce_kernel, nblk),
        out_shape=[jax.ShapeDtypeStruct(b.shape[4:], F32) for b in blocks],
        in_specs=[ANY] * nblk,
        out_specs=[VMEM] * nblk,
        scratch_shapes=scratch(lambda r, w: (2, NZ, NY, r, w))
        + scratch(lambda r, w: (2, NZ, NY, r, w))
        + scratch(lambda r, w: (NZ, NY, r // 2, w))
        + scratch(lambda r, w: (2, NZ, r // 2, w))
        + scratch(lambda r, w: (NZ, r // 2, w))
        + scratch(lambda r, w: (NZ, r // 2, w))
        + scratch(lambda r, w: (2, NZ, r, w))
        + scratch(lambda r, w: (NZ, r, w))
        + scratch(lambda r, w: (NZ, r, w))
        + [
            dma((nblk, 2)), dma((nblk, 2)), dma((nblk, 2)),
            dma((nblk, 2)), dma((nblk, 2)), dma((nblk, 2)), dma((nblk, 2)),
            dma((nblk, 2, NZ)), dma((nblk, 2, NZ)),
        ],
        compiler_params=pltpu.CompilerParams(
            collective_id=2, has_side_effects=True, vmem_limit_bytes=60 << 20
        ),
        name="reduce_grads",
    )(*blocks)


def gelu_exact(values):
    return jax.nn.gelu(values, approximate=False)


def norm_forward(residual, gain_row, shift_row):
    center = jnp.mean(residual, 1)
    spread = lax.rsqrt(jnp.mean(residual * residual, 1) - center * center + EPS)
    normed = (residual - center[:, None]) * spread[:, None]
    return (normed * gain_row + shift_row, normed, spread)


def norm_backward(grad_out, gain_row, normed, spread):
    scaled = grad_out * gain_row
    first_mean = jnp.mean(scaled, 1)
    second_mean = jnp.mean(scaled * normed, 1)
    grad_in = spread[:, None] * (scaled - first_mean[:, None] - normed * second_mean[:, None])
    return (grad_in, jnp.sum(grad_out * normed, 0), jnp.sum(grad_out, 0))


def heads_of(values):
    return values.reshape(values.shape[0], -1, HEAD_DIM)


def layer_forward(residual, halo, weights, keep_masks, same_doc):
    w_q, w_k, w_v, w_proj, w_up, w_down, bias_up, shifts, scales = weights
    own = residual.astype(BF)
    window = jnp.concatenate([halo[0], own, halo[1]], 0)
    queries = heads_of((mm(own, w_q) + shifts[0]).astype(BF))
    keys = heads_of(mm(window, w_k).astype(BF))
    values = heads_of((mm(window, w_v) + shifts[1]).astype(BF))
    scores = jnp.einsum("qhd,khd->hqk", queries, keys, preferred_element_type=F32) * HEAD_DIM**-0.5
    scores = jnp.where(same_doc[None], scores, -1000000000.0)
    row_peak = jnp.max(scores, -1, keepdims=True)
    exponent = jnp.exp(scores - row_peak)
    totals = jnp.sum(exponent, -1, keepdims=True)
    soft_probs = (exponent / totals).astype(BF)
    log_sums = row_peak + jnp.log(totals)
    attended = jnp.einsum("hqk,khd->qhd", soft_probs, values, preferred_element_type=F32)
    attended = attended.astype(BF).reshape(own.shape)
    mixed_out = mm(attended, w_proj) + shifts[2]
    middle, normed_one, spread_one = norm_forward(
        residual + keep_masks[0] * mixed_out / KEEP, scales[0], shifts[3]
    )
    middle_low = middle.astype(BF)
    hidden = mm(middle_low, w_up) + bias_up
    active = gelu_exact(hidden).astype(BF)
    branch = mm(active, w_down) + shifts[4]
    output, normed_two, spread_two = norm_forward(
        middle + keep_masks[1] * branch / KEEP, scales[1], shifts[5]
    )
    saved = (window, queries, keys, values, attended, log_sums, normed_one, spread_one,
             middle_low, hidden, active, normed_two, spread_two)
    return output, saved


def layer_backward(grad_out, weights, keep_masks, saved, same_doc, cid):
    w_q, w_k, w_v, w_proj, w_up, w_down, bias_up, shifts, scales = weights
    (window, queries, keys, values, attended, log_sums, normed_one, spread_one,
     middle_low, hidden, active, normed_two, spread_two) = saved
    rows = grad_out.shape[0]
    grad_two, gain_two, shift_two = norm_backward(grad_out, scales[1], normed_two, spread_two)
    grad_branch = grad_two * keep_masks[1] / KEEP
    bias_down = jnp.sum(grad_branch, 0)
    branch_low = grad_branch.astype(BF)
    grad_active = contract(branch_low, w_down, 1, 1)
    grad_down = contract(active, branch_low, 0, 0).astype(BF)
    grad_hidden = jax.vjp(gelu_exact, hidden)[1](grad_active)[0].astype(BF)
    grad_bias_up = jnp.sum(grad_hidden.astype(F32), 0)
    grad_up = contract(middle_low, grad_hidden, 0, 0).astype(BF)
    grad_middle = grad_two + contract(grad_hidden, w_up, 1, 1)
    grad_one, gain_one, shift_one = norm_backward(grad_middle, scales[0], normed_one, spread_one)
    grad_mixed = grad_one * keep_masks[0] / KEEP
    bias_proj = jnp.sum(grad_mixed, 0)
    mixed_low = grad_mixed.astype(BF)
    grad_proj = contract(attended, mixed_low, 0, 0).astype(BF)
    grad_att = heads_of(contract(mixed_low, w_proj, 1, 1).astype(BF))
    scores = jnp.einsum("qhd,khd->hqk", queries, keys, preferred_element_type=F32) * HEAD_DIM**-0.5
    scores = jnp.where(same_doc[None], scores, -1000000000.0)
    soft_probs = jnp.exp(scores - log_sums)
    grad_v = jnp.einsum("hqk,qhd->khd", soft_probs.astype(BF), grad_att, preferred_element_type=F32)
    grad_probs = jnp.einsum("qhd,khd->hqk", grad_att, values, preferred_element_type=F32)
    inner_sum = jnp.sum(soft_probs * grad_probs, -1, keepdims=True)
    grad_scores = (soft_probs * (grad_probs - inner_sum)).astype(BF)
    grad_q = jnp.einsum("hqk,khd->qhd", grad_scores, keys, preferred_element_type=F32) * HEAD_DIM**-0.5
    grad_k = jnp.einsum("hqk,qhd->khd", grad_scores, queries, preferred_element_type=F32) * HEAD_DIM**-0.5
    grad_q = grad_q.astype(BF).reshape(rows, -1)
    grad_k = grad_k.astype(BF).reshape(window.shape)
    grad_v = grad_v.astype(BF).reshape(window.shape)
    own = window[HALO : HALO + rows]
    grad_wq = contract(own, grad_q, 0, 0).astype(BF)
    grad_wk = contract(window, grad_k, 0, 0).astype(BF)
    grad_wv = contract(window, grad_v, 0, 0).astype(BF)
    grad_window = contract(grad_k, w_k, 1, 1) + contract(grad_v, w_v, 1, 1)
    edges = grad_window.astype(BF)
    swapped = swap_halos(edges[:HALO], edges[HALO + rows :], cid)
    grad_in = grad_one + contract(grad_q, w_q, 1, 1) + grad_window[HALO : HALO + rows]
    grad_in = grad_in + jnp.concatenate([swapped[0], swapped[1]], 0).astype(F32)
    bias_q = jnp.sum(grad_q.astype(F32), 0)
    bias_v = jnp.sum(grad_v.astype(F32), 0)
    grad_shifts = jnp.stack([bias_q, bias_v, bias_proj, shift_one, bias_down, shift_two])
    grad_scales = jnp.stack([gain_one, gain_two])
    return grad_in, (grad_wq, grad_wk, grad_wv, grad_proj, grad_up, grad_down, grad_bias_up, grad_shifts, grad_scales)


def unit_rows(values):
    return values * lax.rsqrt(jnp.sum(values * values, 1, keepdims=True) + EPS)


def per_device(tokens_in, segments, pairing, drop_masks, w_qkv, w_out, w_in, w_back, b_in, biases,
               gains, pool_w, pool_b):
    inner = lax.axis_size("g")
    layers = w_qkv.shape[0]
    width = tokens_in.shape[1]
    local_rows = tokens_in.shape[0]
    z, y, x, c = position()
    m = 2 * x + c
    dp = (z * NY + y) * inner + lax.axis_index("g")

    def group(arr, dim):
        return arr if inner == 1 else lax.all_gather(arr, "g", axis=dim, tiled=True)

    w_qkv, w_out, w_in, w_back = group(w_qkv, 2), group(w_out, 1), group(w_in, 1), group(w_back, 1)
    b_in, biases, gains = group(b_in, 1), group(biases, 2), group(gains, 2)
    pool_w, pool_b, pairing = group(pool_w, 0), group(pool_b, 0), group(pairing, 0)
    rows = w_in.shape[1]
    part = w_qkv.shape[3]
    rows_out = w_out.shape[1]
    fold = width // part
    spare = rows_out * width // (3 * rows)

    side = w_out.reshape(layers, rows_out * fold, 3, spare)
    main = jnp.moveaxis(w_qkv, 1, 2)
    block_a = jnp.concatenate([main, side], 3).reshape(layers, rows, -1)
    smalls = [b_in, biases.reshape(-1, rows), gains.reshape(-1, rows), pool_b[None]]
    smalls = jnp.concatenate([s.astype(F32) for s in smalls], 0)
    smalls = jnp.pad(smalls, ((0, 0), (0, 128 - rows)))
    pair_row = jnp.pad(pairing.astype(F32), (0, 128 - pairing.shape[0]))[None]
    smalls = jnp.concatenate([smalls, pair_row], 0)
    smalls = jnp.pad(smalls, ((0, 24 - smalls.shape[0]), (0, 0)))
    pool_pad = pool_w
    blocks = [smalls]
    for layer in range(layers):
        blocks += [block_a[layer], w_in[layer], w_back[layer]]
    blocks.append(pool_pad)
    full, halo = gather_all(blocks, tokens_in)

    small_full = full[0].reshape(4, NZ * NY, 24, 128)
    wide = small_full[0, :, :, :rows]
    n_b = layers
    n_s = n_b + layers * 6
    n_g = n_s + layers * 2
    bias_up_all = small_full[:, :, :n_b, :rows].transpose(2, 0, 1, 3).reshape(layers, -1)
    shifts_all = wide[:, n_b:n_s].transpose(1, 0, 2).reshape(layers, 6, width)
    scales_all = wide[:, n_s:n_g].transpose(1, 0, 2).reshape(layers, 2, width)
    pool_shift = wide[:, n_g].reshape(width)
    pair_all = small_full[0, :, n_g + 1, : pairing.shape[0]].reshape(-1).astype(jnp.int32)
    pool_full = full[-1][0, 0].reshape(width, width)

    weights = []
    for layer in range(layers):
        a, i, b = full[1 + 3 * layer : 4 + 3 * layer]
        a = a.reshape(4, NZ * NY * rows, 3, part + spare)
        qkv = a[..., :part].transpose(2, 1, 0, 3).reshape(3, width, width)
        proj = a[..., part:].reshape(width, width)
        up = i.reshape(4, width, -1).transpose(1, 0, 2).reshape(width, -1)
        down = b.reshape(-1, width)
        weights.append((qkv[0], qkv[1], qkv[2], proj, up, down, bias_up_all[layer],
                        shifts_all[layer], scales_all[layer]))

    labels = jnp.pad(segments[0], (HALO, HALO), constant_values=-1)
    around = lax.dynamic_slice_in_dim(labels, m * local_rows, local_rows + 2 * HALO, 0)
    mine = around[HALO : HALO + local_rows]
    same_doc = mine[:, None] == around[None, :]
    halo = jnp.stack([jnp.where(m > 0, halo[0], 0), jnp.where(m < 3, halo[1], 0)])
    keep = drop_masks.astype(F32)

    residual = tokens_in.astype(F32)
    saved_all = []
    for layer in range(layers):
        if layer:
            low = residual.astype(BF)
            halo = swap_halos(low[:HALO], low[local_rows - HALO :], 2 + layer)
        residual, saved = layer_forward(residual, halo, weights[layer], keep[layer], same_doc)
        saved_all.append(saved)

    numbers = jnp.arange(SEGS, dtype=jnp.int32)
    starts = jnp.sum((segments[0][None, :] < numbers[:, None]).astype(jnp.int32), 1)
    here = starts[:, None] == (m * local_rows + jnp.arange(local_rows, dtype=jnp.int32))[None, :]
    pick = here.astype(BF)
    shared = share_pooled(mm(pick, residual.astype(BF)).astype(BF))
    cls = shared.reshape(NZ * NY, SEGS, width)
    if inner > 1:
        cls = lax.all_gather(cls, "g", axis=1, tiled=True)
    cls = cls.reshape(-1, width)
    count = cls.shape[0]
    pooled = jnp.tanh(mm(cls, pool_full) + pool_shift)
    normed_pool, unit_back = jax.vjp(unit_rows, pooled)
    unit = normed_pool.astype(BF)
    gram = contract(unit, unit, 1, 1)
    logits = gram / TEMP
    ids = jnp.arange(count, dtype=jnp.int32)
    self_mask = ids[None, :] == ids[:, None]
    pair_mask = ids[None, :] == pair_all[:, None]
    masked = jnp.where(self_mask, -1000000000.0, logits)
    row_peak = jnp.max(masked, 1, keepdims=True)
    exponent = jnp.exp(masked - row_peak)
    totals = jnp.sum(exponent, 1, keepdims=True)
    loss_rows = row_peak[:, 0] + jnp.log(totals[:, 0]) - jnp.sum(jnp.where(pair_mask, logits, 0.0), 1)
    squares = jnp.sum(jnp.square(unit.astype(F32)), 1)
    distance = squares[:, None] + squares[None, :] - 2.0 * gram
    align_rows = jnp.sum(jnp.where(pair_mask, distance, 0.0), 1)
    unif_rows = jnp.log(jnp.sum(jnp.where(self_mask, 0.0, jnp.exp(-2.0 * distance)), 1) / (count - 1))
    grad_raw = ((exponent / totals - pair_mask.astype(F32)) / TEMP).astype(BF)
    grad_unit = contract(grad_raw, unit, 1, 0) + contract(grad_raw, unit, 0, 0)
    grad_pooled = unit_back(grad_unit)[0]
    grad_before = (grad_pooled * (1.0 - pooled * pooled)).astype(BF)
    grad_pool_b = jnp.sum(grad_before.astype(F32), 0)
    rows_pool = width // (NZ * NY * inner)
    cls_cols = lax.dynamic_slice_in_dim(cls, dp * rows_pool, rows_pool, 1)
    grad_pool_w = contract(cls_cols, grad_before, 0, 0)
    grad_pool_b = lax.dynamic_slice_in_dim(grad_pool_b, dp * rows_pool, rows_pool, 0)
    own_before = lax.dynamic_slice_in_dim(grad_before, dp * SEGS, SEGS, 0)
    grad_cls = contract(own_before, pool_full, 1, 1)
    grad_resid = lax.dot_general(
        here.astype(F32), grad_cls, (((0,), (0,)), ((), ())),
        precision=lax.Precision.HIGHEST, preferred_element_type=F32)

    def own_rows(values):
        return lax.dynamic_slice_in_dim(values, dp * SEGS, SEGS, 0)

    grads = [None] * layers
    for layer in reversed(range(layers)):
        grad_resid, grads[layer] = layer_backward(
            grad_resid, weights[layer], keep[layer], saved_all[layer], same_doc, 5 + layer)

    outs_blocks = []
    for layer in reversed(range(layers)):
        g_q, g_k, g_v, g_proj, g_up, g_down = grads[layer][:6]
        qkv = jnp.stack([g_q, g_k, g_v]).reshape(3, width, 4, part).transpose(2, 1, 0, 3)
        proj = g_proj.reshape(4, NZ * NY * rows, 3, spare)
        a = jnp.concatenate([qkv, proj], 3).reshape(2, 2, NZ, NY, rows, -1)
        i = g_up.reshape(width, 4, -1).transpose(1, 0, 2).reshape(2, 2, NZ, NY, rows, -1)
        b = g_down.reshape(2, 2, NZ, NY, -1, width)
        outs_blocks += [b, i, a]
    g_bias = jnp.stack([grads[layer][6] for layer in range(layers)])
    g_shift = jnp.stack([grads[layer][7] for layer in range(layers)])
    g_scale = jnp.stack([grads[layer][8] for layer in range(layers)])
    thin = rows // (4 * inner)

    def sliced(values):
        k = values.shape[1]
        values = values.reshape(layers, k, NZ * NY, inner, 4, thin)
        return values.transpose(4, 2, 0, 1, 3, 5).reshape(4, NZ * NY, -1)

    g_small = jnp.concatenate([
        g_bias.reshape(layers, 4, NZ * NY, rows).transpose(1, 2, 0, 3).reshape(4, NZ * NY, -1),
        sliced(g_shift), sliced(g_scale)], 2)
    n_small = g_small.shape[2]
    g_small = jnp.pad(g_small, ((0, 0), (0, 0), (0, 16 * 128 - n_small)))
    outs_blocks.append(g_small.reshape(2, 2, NZ, NY, 16, 128))
    summed = reduce_all(outs_blocks)

    def spread(values, dim):
        return values if inner == 1 else lax.psum_scatter(values, "g", scatter_dimension=dim, tiled=True)

    out_qkv, out_proj, out_up, out_down = [], [], [], []
    for layer in range(layers):
        at = 3 * (layers - 1 - layer)
        b, i, a = summed[at : at + 3]
        a = a.reshape(rows, 3, part + spare)
        out_qkv.append(spread(jnp.moveaxis(a[..., :part], 1, 0), 1))
        out_proj.append(spread(a[..., part:].reshape(rows_out, width), 0))
        out_up.append(spread(i, 0))
        out_down.append(spread(b, 0))
    flat = summed[-1].reshape(-1)
    e1 = layers * rows
    e2 = e1 + layers * 6 * inner * thin
    e3 = e2 + layers * 2 * inner * thin
    out_b_in = spread(flat[:e1].reshape(layers, rows), 1)
    out_biases = spread(flat[e1:e2].reshape(layers, 6, inner * thin), 2)
    out_gains = spread(flat[e2:e3].reshape(layers, 2, inner * thin), 2)
    return (
        own_rows(loss_rows),
        own_rows(align_rows),
        own_rows(unif_rows),
        grad_resid,
        jnp.stack(out_qkv),
        jnp.stack(out_proj),
        jnp.stack(out_up),
        jnp.stack(out_down),
        out_b_in,
        out_biases,
        out_gains,
        grad_pool_w,
        grad_pool_b,
    )


def solution(mesh):
    count = mesh.shape["dp"]
    fine = Mesh(
        mesh.devices.reshape(NZ, NY, count // (NZ * NY), 2, 2), ("z", "y", "g", "x", "c")
    )
    dp, mp = ("z", "y", "g"), ("x", "c")
    in_specs = (
        P(dp + mp, None),
        P(dp, None),
        P(dp),
        P(None, None, dp + mp, None),
        P(None, None, dp, mp),
        P(None, mp + dp, None),
        P(None, dp, mp),
        P(None, mp + dp, None),
        P(None, mp + dp),
        P(None, None, dp),
        P(None, None, dp),
        P(dp, None),
        P(dp),
    )
    out_specs = (
        P(dp),
        P(dp),
        P(dp),
        P(dp + mp, None),
        P(None, None, dp, mp),
        P(None, mp + dp, None),
        P(None, dp, mp),
        P(None, mp + dp, None),
        P(None, mp + dp),
        P(None, None, dp + mp),
        P(None, None, dp + mp),
        P(dp, None),
        P(dp),
    )
    return jax.shard_map(
        per_device, mesh=fine, in_specs=in_specs, out_specs=out_specs, check_vma=False
    )
```

time: 1540 us -> 868 us (0.56)
  waiting for transfers between devices: 775 us -> 0 us
  blocking collectives: 418 us -> 0 us
  Pallas kernels: 0 us -> 339 us
  local copies, waits for them, and re-layouts: 69.7 us -> 263 us
  matrix products: 148 us -> 166 us
  between operations: 19.3 us -> 3.26 us
    reduce_scatter x15 -> x0, waiting for transfers between devices: 564 us -> none  [the longest x2 141 us: per_device(): lax.psum_scatter(layer_grads[2], 'dp', scatter_dimension=0, tiled=True)]
    pallas_call x0 -> x6, Pallas kernels: none -> 339 us  [the longest x1 163 us: gather_all(): pl.pallas_call(functools.partial(gather_kernel, nblk), out_shape=outs + [...]
    all_gather x9 -> x0, blocking collectives: 298 us -> none  [the longest x2 77.5 us: fetch_layer(): lax.all_gather(w_qkv[layer_index], 'dp', axis=1, tiled=True)]
    all_gather x13 -> x0, waiting for transfers between devices: 125 us -> none  [the longest x8 73.1 us: full_rows(): return lax.all_gather(shard_part, 'mp', axis=0, tiled=True)]
    unnamed x3 -> x0, blocking collectives: 97 us -> none
    reshape x0 -> x22, local copies, waits for them, and re-layouts: none -> 95 us  [the longest x2 26.6 us: per_device(): a = jnp.concatenate([qkv, proj], 3).reshape(2, 2, NZ, NY, rows, -1)]
    unnamed x32 -> x0, waiting for transfers between devices: 86.3 us -> none
    slice x17 -> x23, local copies, waits for them, and re-layouts: 19.2 us -> 68 us  [the longest x4 32.2 us: per_device(): qkv[1]]
  transfers between devices with their start and end apart: 30 -> 0, of which waited for: 21 -> 0; matrix products, arithmetic and copies ran while one was open for 12% -> 0% of each run, Pallas kernels for 0% -> 0%
where the time goes in v1:
time: 868 us; the launch traced here: 857 us
  Pallas kernels  339 us (39%)
  local copies, waits for them, and re-layouts  263 us (30%)
  matrix products  166 us (19%)
  other arithmetic  85.3 us (10%)
    pallas_call x1, Pallas kernels, gather_all(): pl.pallas_call(functools.partial(gather_kernel, nblk), out_shape=outs + [...  163 us
    pallas_call x1, Pallas kernels, reduce_all(): pl.pallas_call(functools.partial(reduce_kernel, nblk), out_shape=[jax.Sha...  149 us
    dot_general x29, matrix products, contract(): lax.dot_general(left_side, right_side, (((left_dim,), (right_dim,)), ((),...  70.2 us
    dot_general x14, matrix products, mm(): return jnp.dot(a, b, preferred_element_type=F32)  57.4 us
    another operation x6, local copies, waits for them, and re-layouts, per_device(): jnp.stack([g_q, g_k, g_v]).reshape(3, width, 4, part).transpose(2, 1, 0, 3)  45.4 us
    slice x4, local copies, waits for them, and re-layouts, per_device(): qkv[1]  32.2 us
    transpose x2, other arithmetic, per_device(): jnp.stack([g_q, g_k, g_v]).reshape(3, width, 4, part).transpose(2, 1, 0, 3)  29.1 us
    reshape x2, local copies, waits for them, and re-layouts, per_device(): a = jnp.concatenate([qkv, proj], 3).reshape(2, 2, NZ, NY, rows, -1)  26.6 us

profile of v1, /device:TPU:0, one launch (start us, length us, event | category | flops | bytes accessed | tf_op | source)
XLA Modules:
  0.0 857.3 jit_solution(9716478664080575581)
XLA Ops:
  7.8 163.2 %gather_params.1 = (f32[2,2,4,2,24,128]{5,4,3,2,1,0:T(8,128)}, bf16[2,2,4,2,96,768]{5,4,3,2,1,0:T(8,128)(2,1)}, bf16[2,2,4,2,96,768]{5,4,3,2,1,0:T(8,128)(2,1)},...) custom-call(f32[24,128]{1,0:T(8,128)} %select_maximum_fusion.2.refs_, ...), custom_call_target="tpu_custom_call" | custom-call | tf_op jit(solution)/shard_map/gather_params/pallas_call | solution.py:230
  172.8 11.5 %reshape.478 = bf16[4,768,3,256]{3,2,1,0:T(4,128)(2,1)} reshape(bf16[2,2,4,2,96,768]{5,4,3,2,1,0:T(8,128)(2,1)} %get-tuple-element.30) | data formatting | bytes 9437184 | tf_op jit(solution)/shard_map/reshape | solution.py:718
  189.2 8.0 fusion.109
  197.2 8.2 copy.94
  254.1 6.7 copy.96
  260.8 11.8 %multiply_convert_fusion.3 = (bf16[256,3072]{1,0:T(8,128)(2,1)}, f32[256,3072]{1,0:T(8,128)}, f32[256,3072]{1,0:T(8,128)}) fusion(f32[3072]{0:T(1024)S(1)} %add.327, bf16[768,3072]{0,1:T(8,128)(2,1)} %bitcast.327, f32[256,768]{1,0:T(8,128)} %get-tuple-element.176, f32[768]{0:T(1024)S(1)} %add.324, f32[768]{0:T(1024)S(1)} %mul.417, ...), kind=kOutput, calls=%fused_computation.55 | convolution fusion | flops 1260847104 | bytes 13389824 | tf_op jit(solution)/shard_map/dot_general | solution.py:36
  285.4 11.7 %reshape.488 = bf16[4,768,3,256]{3,2,1,0:T(4,128)(2,1)} reshape(bf16[2,2,4,2,96,768]{5,4,3,2,1,0:T(8,128)(2,1)} %get-tuple-element.34) | data formatting | bytes 9437184 | tf_op jit(solution)/shard_map/reshape | solution.py:718
  302.1 7.9 fusion.108
  310.0 8.1 copy.101
  356.6 6.8 reshape.493
  368.8 6.6 copy.103
  375.4 11.7 %multiply_convert_fusion.2 = (bf16[256,3072]{1,0:T(8,128)(2,1)}, f32[256,3072]{1,0:T(8,128)}, f32[256,3072]{1,0:T(8,128)}) fusion(f32[3072]{0:T(1024)S(1)} %add.352, bf16[768,3072]{0,1:T(8,128)(2,1)} %bitcast.330, f32[256,768]{1,0:T(8,128)} %get-tuple-element.181, f32[768]{0:T(1024)S(1)} %add.349, f32[768]{0:T(1024)S(1)} %mul.437, ...), kind=kOutput, calls=%fused_computation.42 | convolution fusion | flops 1260847104 | bytes 13389824 | tf_op jit(solution)/shard_map/dot_general | solution.py:36
  387.3 5.4 fusion.101
  395.0 16.1 %share_pooled.1 = bf16[4,2,16,768]{3,2,1,0:T(8,128)(2,1)} custom-call(bf16[16,768]{1,0:T(8,128)(2,1)} %convolution_convert_fusion.16.a_ref), custom_call_target="tpu_custom_call" | custom-call | tf_op jit(solution)/shard_map/share_pooled/pallas_call | solution.py:345
  434.9 6.6 convert_reduce_fusion
  474.6 5.4 convert_reduce_fusion.1
  481.0 5.6 multiply_reduce_fusion.5
  510.0 8.4 copy.114
  521.0 5.5 copy.113
  529.2 8.3 copy.112
  537.4 14.5 %maximum_bitcast_fusion.1 = bf16[4,768,3,192]{3,2,1,0:T(4,128)(2,1)} fusion(bf16[1,768,4,192]{3,0,1,2:T(2,128)(2,1)S(1)} %copy-done.10, bf16[1,768,4,192]{3,0,1,2:T(2,128)(2,1)} %copy.113, bf16[1,768,4,192]{3,0,1,2:T(2,128)(2,1)} %copy.112), kind=kLoop, calls=%fused_computation.4 | loop fusion | flops 10616832 | bytes 7077888 | tf_op jit(solution)/shard_map/transpose | solution.py:795
  553.5 5.9 reshape.513
  559.4 11.0 %pad_maximum_fusion.1 = bf16[4,768,3,256]{3,2,1,0:T(4,128)(2,1)} fusion(bf16[4,768,3,64]{3,2,1,0:T(4,128)(2,1)S(1)} %reshape.513, bf16[4,768,3,192]{3,2,1,0:T(4,128)(2,1)} %maximum_bitcast_fusion.1), kind=kLoop, calls=%fused_computation.5 | loop fusion | flops 9437184 | bytes 9437184 | tf_op jit(solution)/shard_map/concatenate | solution.py:797
  570.4 13.2 %reshape.514.refs_5_ = bf16[2,2,4,2,96,768]{5,4,3,2,1,0:T(8,128)(2,1)} reshape(bf16[4,768,3,256]{3,2,1,0:T(4,128)(2,1)} %pad_maximum_fusion.1) | data formatting | bytes 9437184 | tf_op jit(solution)/shard_map/reshape | solution.py:797
  592.8 6.7 copy.108
  602.7 8.3 copy.109
  614.1 8.3 copy.110
  622.4 14.6 %maximum_bitcast_fusion = bf16[4,768,3,192]{3,2,1,0:T(4,128)(2,1)} fusion(bf16[1,768,4,192]{3,0,1,2:T(2,128)(2,1)} %copy.110, bf16[1,768,4,192]{3,0,1,2:T(2,128)(2,1)} %copy.109, bf16[1,768,4,192]{3,0,1,2:T(2,128)(2,1)S(1)} %copy.108), kind=kLoop, calls=%fused_computation.2 | loop fusion | flops 10616832 | bytes 7077888 | tf_op jit(solution)/shard_map/transpose | solution.py:795
  638.4 5.7 reshape.508
  644.2 11.0 %pad_maximum_fusion = bf16[4,768,3,256]{3,2,1,0:T(4,128)(2,1)} fusion(bf16[4,768,3,64]{3,2,1,0:T(4,128)(2,1)S(1)} %reshape.508, bf16[4,768,3,192]{3,2,1,0:T(4,128)(2,1)} %maximum_bitcast_fusion), kind=kLoop, calls=%fused_computation.3 | loop fusion | flops 9437184 | bytes 9437184 | tf_op jit(solution)/shard_map/concatenate | solution.py:797
  655.2 13.4 %reshape.509.refs_2_ = bf16[2,2,4,2,96,768]{5,4,3,2,1,0:T(8,128)(2,1)} reshape(bf16[4,768,3,256]{3,2,1,0:T(4,128)(2,1)} %pad_maximum_fusion) | data formatting | bytes 9437184 | tf_op jit(solution)/shard_map/reshape | solution.py:797
  676.4 148.8 %reduce_grads.1 = (f32[96,768]{1,0:T(8,128)}, f32[96,768]{1,0:T(8,128)}, f32[96,768]{1,0:T(8,128)}, f32[96,768]{1,0:T(8,128)}, f32[96,768]{1,0:T(8,128)}, /*index=5*/f32[96,768]{1,0:T(8,128)}, f32[16,128]{1,0:T(8,128)}) custom-call(bf16[2,2,4,2,96,768]{5,4,3,2,1,0:T(8,128)(2,1)} %bitcast.316, bf16[2,2,4,2,96,768]{5,4,3,2,1,0:T(8,128)(2,1)} %bitcast.320, ...), custom_call_target="tpu_custom_call" | custom-call | tf_op jit(solution)/shard_map/reduce_grads/pallas_call | solution.py:531
  (551 shorter events, 269.3 us)
Async XLA Ops:
  223.6 12.1 %copy-start.77 = (f32[12,256]{1,0:T(8,128)}, f32[12,256]{1,0:T(8,128)S(1)}, u32[]{:S(2)}) copy-start(f32[12,256]{1,0:T(8,128)S(1)} %get-tuple-element.174) | copy-start | bytes 36868
  250.3 22.3 %copy-start.2 = (f32[2,2,256,768]{3,2,1,0:T(8,128)}, f32[2,2,256,768]{3,2,1,0:T(8,128)S(1)}, u32[]{:S(2)}) copy-start(f32[2,2,256,768]{3,2,1,0:T(8,128)S(1)} %convert_element_type.275) | copy-start | bytes 9437188
  252.2 20.4 %copy-start.114 = (f32[256]{0:T(256)}, f32[256]{0:T(256)S(1)}, u32[]{:S(2)}) copy-start(f32[256]{0:T(256)S(1)} %get-tuple-element.172) | copy-start | bytes 3076
  252.2 20.4 %copy-start.117 = (f32[256]{0:T(256)}, f32[256]{0:T(256)S(1)}, u32[]{:S(2)}) copy-start(f32[256]{0:T(256)S(1)} %get-tuple-element.173) | copy-start | bytes 3076
  260.8 11.8 %copy-start.108 = (f32[8,96]{1,0:T(8,128)S(1)}, f32[8,96]{1,0:T(8,128)}, u32[]{:S(2)}) copy-start(f32[8,96]{1,0:T(8,128)} %get-tuple-element.110) | copy-start | bytes 9220
  278.0 85.4 %copy-start.91 = (f32[256]{0:T(256)}, f32[256]{0:T(256)S(1)}, u32[]{:S(2)}) copy-start(f32[256]{0:T(256)S(1)} %get-tuple-element.170) | copy-start | bytes 3076
  278.1 85.3 %copy-start.82 = (f32[768]{0:T(1024)}, f32[768]{0:T(1024)S(1)}, u32[]{:S(2)}) copy-start(f32[768]{0:T(1024)S(1)} %mul.428) | copy-start | bytes 9220
  279.5 64.5 %copy-start.32 = (bf16[256,768]{1,0:T(8,128)(2,1)}, bf16[256,768]{1,0:T(8,128)(2,1)S(1)}, u32[]{:S(2)}) copy-start(bf16[256,768]{1,0:T(8,128)(2,1)S(1)} %fusion.54) | copy-start | bytes 1179652
  350.7 12.8 %copy-start.68 = (bf16[12,64,256]{2,1,0:T(8,128)(2,1)}, bf16[12,64,256]{2,1,0:T(8,128)(2,1)S(1)}, u32[]{:S(2)}) copy-start(bf16[12,64,256]{2,1,0:T(8,128)(2,1)S(1)} %fusion.50) | copy-start | bytes 1179652
  366.5 20.7 %copy-start.120 = (f32[256]{0:T(256)}, f32[256]{0:T(256)S(1)}, u32[]{:S(2)}) copy-start(f32[256]{0:T(256)S(1)} %get-tuple-element.168) | copy-start | bytes 3076
  366.5 20.7 %copy-start.123 = (f32[256]{0:T(256)}, f32[256]{0:T(256)S(1)}, u32[]{:S(2)}) copy-start(f32[256]{0:T(256)S(1)} %get-tuple-element.169) | copy-start | bytes 3076
  375.4 11.7 %copy-start.104 = (f32[8,96]{1,0:T(8,128)S(1)}, f32[8,96]{1,0:T(8,128)}, u32[]{:S(2)}) copy-start(f32[8,96]{1,0:T(8,128)} %get-tuple-element.104) | copy-start | bytes 9220
  392.6 21.2 %copy-start.128 = (f32[256]{0:T(256)}, f32[256]{0:T(256)S(1)}, u32[]{:S(2)}) copy-start(f32[256]{0:T(256)S(1)} %get-tuple-element.166) | copy-start | bytes 3076
  392.6 21.2 %copy-start.129 = (f32[256]{0:T(256)}, f32[256]{0:T(256)S(1)}, u32[]{:S(2)}) copy-start(f32[256]{0:T(256)S(1)} %get-tuple-element.167) | copy-start | bytes 3076
  392.7 21.2 %copy-start.88 = (f32[768]{0:T(1024)}, f32[768]{0:T(1024)S(1)}, u32[]{:S(2)}) copy-start(f32[768]{0:T(1024)S(1)} %mul.448) | copy-start | bytes 9220
  392.8 21.1 %copy-start.142 = (s32[256]{0:T(256)}, s32[256]{0:T(256)S(1)}, u32[]{:S(2)}) copy-start(s32[256]{0:T(256)S(1)} %iota_add_fusion) | copy-start | bytes 3076
  392.9 21.0 %copy-start.141 = (s32[16]{0:T(128)}, s32[16]{0:T(128)S(1)}, u32[]{:S(2)}) copy-start(s32[16]{0:T(128)S(1)} %convert_reduce_fusion.7) | copy-start | bytes 196
  526.5 10.9 %copy-start.10 = (bf16[1,768,4,192]{3,0,1,2:T(2,128)(2,1)S(1)}, bf16[1,768,4,192]{3,0,1,2:T(2,128)(2,1)}, u32[]{:S(2)}) copy-start(bf16[1,768,4,192]{3,0,1,2:T(2,128)(2,1)} %copy.114) | copy-start | bytes 3538948
  537.4 14.5 %copy-start.41 = (bf16[256,768]{1,0:T(8,128)(2,1)S(1)}, bf16[256,768]{1,0:T(8,128)(2,1)}, u32[]{:S(2)}) copy-start(bf16[256,768]{1,0:T(8,128)(2,1)} %copy-done.40) | copy-start | bytes 1179652
  537.4 14.5 %copy-start.67 = (bf16[12,64,256]{2,1,0:T(8,128)(2,1)S(1)}, bf16[12,64,256]{2,1,0:T(8,128)(2,1)}, u32[]{:S(2)}) copy-start(bf16[12,64,256]{2,1,0:T(8,128)(2,1)} %fusion.51) | copy-start | bytes 1179652
  570.4 13.2 %copy-start.27 = (f32[256,768]{1,0:T(8,128)S(1)}, f32[256,768]{1,0:T(8,128)}, u32[]{:S(2)}) copy-start(f32[256,768]{1,0:T(8,128)} %get-tuple-element.176) | copy-start | bytes 2359300
  570.4 13.2 %copy-start.60 = (bf16[256,3072]{1,0:T(8,128)(2,1)S(1)}, bf16[256,3072]{1,0:T(8,128)(2,1)}, u32[]{:S(2)}) copy-start(bf16[256,3072]{1,0:T(8,128)(2,1)} %get-tuple-element.124) | copy-start | bytes 4718596
  570.4 13.2 %copy-start.116 = (f32[256]{0:T(256)S(1)}, f32[256]{0:T(256)}, u32[]{:S(2)}) copy-start(f32[256]{0:T(256)} %copy-done.114) | copy-start | bytes 3076
  570.4 13.2 %copy-start.119 = (f32[256]{0:T(256)S(1)}, f32[256]{0:T(256)}, u32[]{:S(2)}) copy-start(f32[256]{0:T(256)} %copy-done.117) | copy-start | bytes 3076
  622.4 14.6 %copy-start.37 = (bf16[256,768]{1,0:T(8,128)(2,1)S(1)}, bf16[256,768]{1,0:T(8,128)(2,1)}, u32[]{:S(2)}) copy-start(bf16[256,768]{1,0:T(8,128)(2,1)} %copy-done.36) | copy-start | bytes 1179652
  622.4 14.6 %copy-start.69 = (bf16[12,64,256]{2,1,0:T(8,128)(2,1)S(1)}, bf16[12,64,256]{2,1,0:T(8,128)(2,1)}, u32[]{:S(2)}) copy-start(bf16[12,64,256]{2,1,0:T(8,128)(2,1)} %copy-done.68) | copy-start | bytes 1179652
  655.2 13.4 %copy-start.29 = (f32[256,768]{1,0:T(8,128)S(1)}, f32[256,768]{1,0:T(8,128)}, u32[]{:S(2)}) copy-start(f32[256,768]{1,0:T(8,128)} %get-tuple-element.181) | copy-start | bytes 2359300
  655.2 13.4 %copy-start.59 = (bf16[256,3072]{1,0:T(8,128)(2,1)S(1)}, bf16[256,3072]{1,0:T(8,128)(2,1)}, u32[]{:S(2)}) copy-start(bf16[256,3072]{1,0:T(8,128)(2,1)} %copy-done.58) | copy-start | bytes 4718596
  655.2 13.4 %copy-start.122 = (f32[256]{0:T(256)S(1)}, f32[256]{0:T(256)}, u32[]{:S(2)}) copy-start(f32[256]{0:T(256)} %copy-done.120) | copy-start | bytes 3076
  655.2 13.4 %copy-start.125 = (f32[256]{0:T(256)S(1)}, f32[256]{0:T(256)}, u32[]{:S(2)}) copy-start(f32[256]{0:T(256)} %copy-done.123) | copy-start | bytes 3076
  845.6 10.6 %copy-start.126 = (f32[128]{0:T(128)S(1)}, f32[128]{0:T(128)}, u32[]{:S(2)}) copy-start(f32[128]{0:T(128)} %get-tuple-element.186) | copy-start | bytes 1540
  845.6 10.6 %copy-start.131 = (f32[128]{0:T(128)S(1)}, f32[128]{0:T(128)}, u32[]{:S(2)}) copy-start(f32[128]{0:T(128)} %copy-done.130) | copy-start | bytes 1540
  (128 other events, 538.3 us)
